TPU v7x, 32 devices: a whole 2x2x4 slice. The times are simulated.
32 devices in a mesh: pair: 4 (over y, x), blk: 8 (over z, core).
Axes of the slice: x: 2, y: 2, z: 4, core: 2. Of those that a mesh axis runs over, the one named last changes fastest.
Arguments:
- source: bfloat16 [8192, 1024], P(('pair', 'blk'))
- source_label: int32 [8192], P(('pair', 'blk')), may hold values from 0 to 3, as said below
- target: bfloat16 [8192, 1024], P(('pair', 'blk'))
- target_label: int32 [8192], P(('pair', 'blk')), may hold values from 0 to 3, as said below
Outputs:
- src_partner: float32 [8192, 1024], P(('pair', 'blk'))
- src_margin: float32 [8192], P(('pair', 'blk'))
- tgt_margin: float32 [8192], P(('pair', 'blk'))
Inputs may be any that keep to these rules, and one draw needn't show every extreme that they name: `source_label`: rows (i * 8 + k) * 256 to (i * 8 + k + 1) * 256 - 1 form block (i, k). For every k below 4, blocks (i, k) and (i, k + 4) together name every bucket exactly 128 times, so a block names one bucket at most 128 times, and in every draw some block names one bucket 128 times. `target_label`: rows (i * 8 + k) * 256 to (i * 8 + k + 1) * 256 - 1 form block (i, k). For every k below 4, blocks (i, k) and (i, k + 4) together name every bucket exactly 128 times, so a block names one bucket at most 128 times, and in every draw some block names one bucket 128 times.
All inputs are finite; a program needn't handle non-finite values.
Results may differ from a plain program's by a relative error of at most 0.0041.
Values may be sent and summed in bfloat16 or wider, within the bound.
A program may use at most 128 MiB of HBM per device.

v0:
```python
import jax
import jax.numpy as jnp
from jax import lax
from jax.sharding import PartitionSpec as P

sharpness = 12.0


def normalize(row_block):
    values = row_block.astype(jnp.float32)
    square = jnp.mean(values * values, axis=-1, keepdims=True)
    return (values * lax.rsqrt(square + 1e-06)).astype(jnp.bfloat16)


def place_rows(labels, buckets, capacity):
    onehot = (labels[:, None] == jnp.arange(buckets, dtype=jnp.int32)[None, :]).astype(jnp.int32)
    before = jnp.cumsum(onehot, axis=0) - onehot
    slot_rank = jnp.sum(before * onehot, axis=1)
    return (labels * capacity + slot_rank, jnp.sum(onehot, axis=0))


def pack_rows(normed, slot_of, slot_total):
    return jnp.zeros((slot_total, normed.shape[1]), normed.dtype).at[slot_of].set(normed)


def safe_ratio(numer, denom):
    return numer / jnp.where(denom > 0.0, denom, 1.0)


def block_rows(length):
    best_size = 1
    for option in range(1, min(length, 512) + 1):
        if length % option == 0:
            best_size = option
    return best_size


def on_device(source, source_label, target, target_label):
    width = source.shape[1]
    own_rows = source.shape[0]
    buckets = lax.axis_size("pair")
    columns = lax.axis_size("blk")
    capacity = 2 * own_rows // buckets
    slot_total = buckets * capacity
    src_norm = normalize(source)
    tgt_norm = normalize(target)
    src_slot, src_count = place_rows(source_label, buckets, capacity)
    tgt_slot, tgt_count = place_rows(target_label, buckets, capacity)
    src_pack = pack_rows(src_norm, src_slot, slot_total).reshape(buckets, capacity, width)
    tgt_pack = pack_rows(tgt_norm, tgt_slot, slot_total).reshape(buckets, capacity, width)
    src_recv, tgt_recv, src_heard, tgt_heard = (
        lax.all_to_all(src_pack, "pair", split_axis=0, concat_axis=0, tiled=True),
        lax.all_to_all(tgt_pack, "pair", split_axis=0, concat_axis=0, tiled=True),
        lax.all_to_all(src_count, "pair", split_axis=0, concat_axis=0, tiled=True),
        lax.all_to_all(tgt_count, "pair", split_axis=0, concat_axis=0, tiled=True),
    )
    src_slots = src_recv.reshape(slot_total, width)
    tgt_slots = tgt_recv.reshape(slot_total, width)
    cap_spots = jnp.arange(capacity, dtype=jnp.int32)
    src_live = (cap_spots[None, :] < src_heard[:, None]).reshape(slot_total)
    tgt_live = (cap_spots[None, :] < tgt_heard[:, None]).reshape(slot_total)
    stay_live = src_live.astype(jnp.float32)
    move_live = tgt_live.astype(jnp.bfloat16)
    block_count = src_slots.shape[0]
    total_rows = columns * block_count

    def tile_weight(rows_block, live_block):
        similar = (
            lax.dot_general(
                src_slots, rows_block, (((1,), (1,)), ((), ())), preferred_element_type=jnp.float32
            )
            / width
        )
        weight = jnp.exp(sharpness * similar) * (
            stay_live[:, None] * live_block.astype(jnp.float32)[None, :]
        )
        return (similar, weight)

    zeros_rows = jnp.zeros((block_count,), jnp.float32)
    zeros_every = jnp.zeros((total_rows,), jnp.float32)
    held_init = jnp.zeros((1, 1), jnp.float32)
    first_init = (
        jnp.zeros((block_count, width), jnp.float32),
        zeros_rows,
        zeros_rows,
        zeros_every,
        zeros_every,
        held_init,
    )
    first_row = jnp.int32(0)
    part_rows = lax.all_gather(tgt_slots, "blk", axis=0, tiled=True)
    part_live = lax.all_gather(move_live, "blk", axis=0, tiled=True)
    length = part_rows.shape[0]
    step_rows = block_rows(length)

    def first_inner_step(block_index, state):
        partner_acc, fwd_total, fwd_sum, bwd_total, bwd_sum, held_tiles = state
        offset = block_index * step_rows
        rows_block = lax.dynamic_slice_in_dim(part_rows, offset, step_rows, 0)
        live_block = lax.dynamic_slice_in_dim(part_live, offset, step_rows, 0)
        similar, weight = tile_weight(rows_block, live_block)
        weighted = weight * similar
        partner_acc = partner_acc + jnp.dot(
            weight.astype(jnp.bfloat16), rows_block, preferred_element_type=jnp.float32
        )
        fwd_total = fwd_total + jnp.sum(weight, axis=1)
        fwd_sum = fwd_sum + jnp.sum(weighted, axis=1)
        bwd_total = lax.dynamic_update_slice_in_dim(
            bwd_total, jnp.sum(weight, axis=0), first_row + offset, 0
        )
        bwd_sum = lax.dynamic_update_slice_in_dim(
            bwd_sum, jnp.sum(weighted, axis=0), first_row + offset, 0
        )
        return (partner_acc, fwd_total, fwd_sum, bwd_total, bwd_sum, held_tiles)

    partner_acc, fwd_total, fwd_sum, part_total, part_sum, held_tiles = lax.fori_loop(
        0, length // step_rows, first_inner_step, first_init
    )
    summed_total, summed_weighted = lax.psum((part_total, part_sum), "blk")
    bwd_every = safe_ratio(summed_weighted, summed_total)
    own_index = lax.axis_index("blk")
    own_total = lax.dynamic_slice_in_dim(summed_total, own_index * block_count, block_count, 0)
    own_bwd = lax.dynamic_slice_in_dim(bwd_every, own_index * block_count, block_count, 0)
    fwd_stat = safe_ratio(fwd_sum, fwd_total)
    second_first_row = jnp.int32(0)
    second_part_rows = lax.all_gather(tgt_slots, "blk", axis=0, tiled=True)
    second_part_live = lax.all_gather(move_live, "blk", axis=0, tiled=True)
    length = second_part_rows.shape[0]
    second_step_rows = block_rows(length)

    def second_inner_step(block_index, state):
        back_acc, fore_part = state
        offset = block_index * second_step_rows
        rows_block = lax.dynamic_slice_in_dim(second_part_rows, offset, second_step_rows, 0)
        live_block = lax.dynamic_slice_in_dim(second_part_live, offset, second_step_rows, 0)
        similar, weight = tile_weight(rows_block, live_block)
        bwd_block = lax.dynamic_slice_in_dim(
            bwd_every, second_first_row + offset, second_step_rows, 0
        )
        back_acc = back_acc + jnp.dot(weight, bwd_block, precision=lax.Precision.HIGHEST)
        fore_block = jnp.dot(fwd_stat, weight, precision=lax.Precision.HIGHEST)
        fore_part = lax.dynamic_update_slice_in_dim(
            fore_part, fore_block, second_first_row + offset, 0
        )
        return (back_acc, fore_part)

    back_acc, fore_part = lax.fori_loop(
        0, length // second_step_rows, second_inner_step, (zeros_rows, zeros_every)
    )
    fore_own = lax.psum_scatter(
        fore_part.reshape(columns, block_count), "blk", scatter_dimension=0, tiled=True
    )[0]
    partner = safe_ratio(partner_acc, fwd_total[:, None])
    src_margin = fwd_stat - 0.5 * (fwd_stat + safe_ratio(back_acc, fwd_total))
    tgt_margin = own_bwd - 0.5 * (own_bwd + safe_ratio(fore_own, own_total))
    back_partner, back_src, back_tgt = (
        lax.all_to_all(
            partner.reshape(buckets, capacity, width),
            "pair",
            split_axis=0,
            concat_axis=0,
            tiled=True,
        ),
        lax.all_to_all(
            src_margin.reshape(buckets, capacity), "pair", split_axis=0, concat_axis=0, tiled=True
        ),
        lax.all_to_all(
            tgt_margin.reshape(buckets, capacity), "pair", split_axis=0, concat_axis=0, tiled=True
        ),
    )
    partner_out = back_partner.reshape(slot_total, width)[src_slot]
    src_out = back_src.reshape(slot_total)[src_slot]
    tgt_out = back_tgt.reshape(slot_total)[tgt_slot]
    return (partner_out, src_out, tgt_out)


def solution(mesh):
    return jax.shard_map(
        on_device,
        mesh=mesh,
        in_specs=(
            P(("pair", "blk"), None),
            P(("pair", "blk")),
            P(("pair", "blk"), None),
            P(("pair", "blk")),
        ),
        out_specs=(P(("pair", "blk"), None), P(("pair", "blk")), P(("pair", "blk"))),
        check_vma=False,
    )
```

profile of v0, /device:TPU:0, one launch (start us, length us, event | category | flops | bytes accessed | tf_op | source)
XLA Modules:
  0.0 297.8 jit_solution(2852079878491958526)
XLA Ops:
  7.2 0.7 compare_convert_fusion.1
  7.9 1.2 reduce-window.14
  9.5 0.8 convert_reduce_fusion.1
  10.3 0.7 compare_select_fusion.4
  11.0 1.2 fusion.24
  12.2 2.5 scatter_custom_fusion
  14.8 19.2 %all_to_all.51 = bf16[4,128,1024]{2,1,0:T(8,128)(2,1)} all-to-all(bf16[4,128,1024]{2,1,0:T(8,128)(2,1)S(1)} %bitcast.116), channel_id=1, replica_groups=mesh['pair'=4,'blk'=8] {'pair'}, dimensions={0} | all-to-all | bytes 2097152 | tf_op jit(solution)/shard_map/all_to_all | solution.py:53
  34.0 0.7 copy.25
  34.7 3.2 %all-to-all-start.3 = ((s32[4,1,1]{2,1,0:T(1,128)}), s32[4,1,1]{2,1,0:T(1,128)S(1)}, u32[]{:S(2)}, u32[]{:S(2)}) async-start(s32[4,1,1]{2,1,0:T(1,128)} %copy.25), calls=%async_computation.3 | async-start | bytes 4096 | tf_op jit(solution)/shard_map/all_to_all | solution.py:55
  37.9 1.2 reduce-window.16
  40.0 2.7 scatter_custom_fusion.1
  42.7 8.6 %all_to_all.52 = s32[4,1,1]{2,1,0:T(1,128)S(1)} all-to-all(s32[4,1,1]{2,1,0:T(1,128)S(1)} %copy.26), channel_id=1, replica_groups=mesh['pair'=4,'blk'=8] {'pair'}, dimensions={0} | all-to-all | bytes 32 | tf_op jit(solution)/shard_map/all_to_all | solution.py:54
  51.3 4.3 %all-to-all-start.1 = ((bf16[4,128,1024]{2,1,0:T(8,128)(2,1)}), bf16[4,128,1024]{2,1,0:T(8,128)(2,1)}, u32[]{:S(2)}, u32[]{:S(2)}) async-start(bf16[4,128,1024]{2,1,0:T(8,128)(2,1)} %bitcast.8), calls=%async_computation.1 | async-start | bytes 2097152 | tf_op jit(solution)/shard_map/all_to_all | solution.py:52
  56.5 16.0 %all-gather = bf16[8,1,512]{2,1,0:T(2,128)(2,1)S(1)} all-gather(bf16[1,1,512]{2,1,0:T(2,128)(2,1)S(1)} %reshape.176), channel_id=1, replica_groups=mesh['pair'=4,'blk'=8] {'blk'}, dimensions={0}, use_global_device_ids=true | all-gather | bytes 9216 | tf_op jit(solution)/shard_map/all_gather | solution.py:92
  72.7 43.4 %all-gather.3.cloned.1.call-done = bf16[4096,1024]{1,0:T(8,128)(2,1)} async-done(((bf16[512,1024]{1,0:T(8,128)(2,1)}), bf16[4096,1024]{1,0:T(8,128)(2,1)}) %all-gather.3.cloned.1.call-update) | async-done | bytes 8388624 | tf_op jit(solution)/shard_map/all_gather | solution.py:91
  116.0 45.0 %while.42 = (s32[]{:T(128)}, f32[512,1024]{1,0:T(8,128)S(1)}, f32[512]{0:T(512)S(1)}, f32[512]{0:T(512)S(1)}, f32[4096]{0:T(1024)S(1)}, /*index=5*/f32[4096]{0:T...) while((s32[]{:T(128)}, f32[512,1024]{1,0:T(8,128)S(1)}, ...), condition=%wide.region_17.18_spmd.clone, body=%wide.region_12.17_spmd.clone.sunk | while | flops 1078199808 | bytes 9479394 | solution.py:116
  116.2 2.6 fusion.69
  118.8 2.3 select_add_fusion.7
  121.8 2.6 fusion.69
  124.5 2.3 select_add_fusion.7
  127.5 2.6 fusion.69
  130.1 2.3 select_add_fusion.7
  133.1 2.6 fusion.69
  135.8 2.3 select_add_fusion.7
  138.8 2.6 fusion.69
  141.4 2.3 select_add_fusion.7
  144.4 2.6 fusion.69
  147.0 2.3 select_add_fusion.7
  150.0 2.6 fusion.69
  152.7 2.3 select_add_fusion.7
  155.6 2.6 fusion.69
  158.2 2.3 select_add_fusion.7
  161.0 26.3 %all-reduce.1 = (f32[4096]{0:T(1024)S(1)}, f32[4096]{0:T(1024)S(1)}) all-reduce(f32[4096]{0:T(1024)S(1)} %get-tuple-element.473, f32[4096]{0:T(1024)S(1)} %get-tuple-element.474), channel_id=1, replica_groups=mesh['pair'=4,'blk'=8] {'blk'}, use_global_device_ids=true, to_apply=%region_18.19 | all-reduce | flops 8192 | bytes 65536 | tf_op jit(solution)/shard_map/psum | solution.py:119
  187.3 35.3 %while.43 = (s32[]{:T(128)}, f32[512]{0:T(512)S(1)}, f32[4096]{0:T(1024)S(1)}, bf16[4096,1024]{1,0:T(8,128)(2,1)}, bf16[512,1024]{1,0:T(8,128)(2,1)}, /*index=5*...) while((s32[]{:T(128)}, f32[512]{0:T(512)S(1)}, ...), condition=%wide.region_21.22_spmd.clone, body=%wide.region_20.21_spmd.clone.sunk | while | flops 543951360 | bytes 5274837 | solution.py:147
  187.5 2.3 fusion.76
  189.8 1.0 fusion.78
  191.9 2.3 fusion.76
  194.2 1.0 fusion.78
  196.3 2.3 fusion.76
  198.6 1.0 fusion.78
  200.7 2.3 fusion.76
  203.1 1.0 fusion.78
  205.1 2.3 fusion.76
  207.5 1.0 fusion.78
  209.6 2.3 fusion.76
  211.9 1.0 fusion.78
  214.0 2.3 fusion.76
  216.3 1.0 fusion.78
  218.4 2.3 fusion.76
  220.7 1.0 fusion.78
  221.9 0.7 fusion.77
  222.6 25.9 %all-reduce = f32[8,512]{1,0:T(8,128)S(1)} all-reduce(f32[8,512]{1,0:T(8,128)S(1)} %reshape.127), channel_id=2, replica_groups=mesh['pair'=4,'blk'=8] {'blk'}, use_global_device_ids=true, to_apply=%region_22.23.clone | all-reduce | flops 4096 | bytes 32768
  248.5 0.7 constant_dynamic-slice_fusion
  249.2 0.7 multiply_subtract_fusion
  249.9 3.9 %all-to-all-start.6 = ((f32[4,1,128]{2,1,0:T(1,128)}), f32[4,1,128]{2,1,0:T(1,128)S(1)}, u32[]{:S(2)}, u32[]{:S(2)}) async-start(f32[4,1,128]{2,1,0:T(1,128)} %bitcast.17), calls=%async_computation.6 | async-start | bytes 4096 | tf_op jit(solution)/shard_map/all_to_all | solution.py:167
  254.4 3.9 %all-to-all-done.6 = f32[4,1,128]{2,1,0:T(1,128)S(1)} async-done(((f32[4,1,128]{2,1,0:T(1,128)}), f32[4,1,128]{2,1,0:T(1,128)S(1)}, u32[]{:S(2)}, u32[]{:S(2)}) %all-to-all-start.6) | async-done | bytes 2080 | tf_op jit(solution)/shard_map/all_to_all | solution.py:167
  258.3 3.2 %all-to-all-start.5 = ((f32[4,1,128]{2,1,0:T(1,128)}), f32[4,1,128]{2,1,0:T(1,128)S(1)}, u32[]{:S(2)}, u32[]{:S(2)}) async-start(f32[4,1,128]{2,1,0:T(1,128)} %bitcast.14), calls=%async_computation.5 | async-start | bytes 4096 | tf_op jit(solution)/shard_map/all_to_all | solution.py:164
  261.5 1.6 broadcast_divide_fusion
  263.1 2.9 all-to-all-done.5
  266.0 3.6 %all-to-all-start.4 = ((f32[4,128,1024]{2,1,0:T(8,128)}), f32[4,128,1024]{2,1,0:T(8,128)S(1)}, u32[]{:S(2)}, u32[]{:S(2)}) async-start(f32[4,128,1024]{2,1,0:T(8,128)} %bitcast.114), calls=%async_computation.4 | async-start | bytes 4194304 | tf_op jit(solution)/shard_map/all_to_all | solution.py:157
  269.7 2.5 gather_fusion.2
  272.2 2.5 gather_fusion.1
  274.7 14.3 %all-to-all-done.4 = f32[4,128,1024]{2,1,0:T(8,128)S(1)} async-done(((f32[4,128,1024]{2,1,0:T(8,128)}), f32[4,128,1024]{2,1,0:T(8,128)S(1)}, u32[]{:S(2)}, u32[]{:S(2)}) %all-to-all-start.4) | async-done | bytes 2097184 | tf_op jit(solution)/shard_map/all_to_all | solution.py:157
  288.9 2.0 gather_fusion
  (136 shorter events, 16.4 us)
Async XLA Ops:
  7.2 108.9 %all-gather.3.cloned.1.call-start = ((), (), s32[]{:S(2)}) async-start(), calls=%async_computation.7 | async-start | bytes 9437184 | tf_op jit(solution)/shard_map/all_gather | solution.py:91
  12.2 25.7 %copy-start.1 = (s32[256]{0:T(256)S(1)}, s32[256]{0:T(256)}, u32[]{:S(2)}) copy-start(s32[256]{0:T(256)} %param.9) | copy-start | bytes 3076
  12.2 27.5 %copy-start = (bf16[256,1024]{1,0:T(8,128)(2,1)S(1)}, bf16[256,1024]{1,0:T(8,128)(2,1)}, u32[]{:S(2)}) copy-start(bf16[256,1024]{1,0:T(8,128)(2,1)} %param.8) | copy-start | bytes 1572868
  34.7 8.0 %all-to-all-start.3 = ((s32[4,1,1]{2,1,0:T(1,128)}), s32[4,1,1]{2,1,0:T(1,128)S(1)}, u32[]{:S(2)}, u32[]{:S(2)}) async-start(s32[4,1,1]{2,1,0:T(1,128)} %copy.25), calls=%async_computation.3 | async-start | bytes 4096 | tf_op jit(solution)/shard_map/all_to_all | solution.py:55
  39.8 15.8 %copy-start.2 = (u32[32]{0:T(128)S(1)}, u32[32]{0:T(128)}, u32[]{:S(2)}) copy-start(u32[32]{0:T(128)} %constant.168) | copy-start | bytes 388
  51.3 21.4 %all-to-all-start.1 = ((bf16[4,128,1024]{2,1,0:T(8,128)(2,1)}), bf16[4,128,1024]{2,1,0:T(8,128)(2,1)}, u32[]{:S(2)}, u32[]{:S(2)}) async-start(bf16[4,128,1024]{2,1,0:T(8,128)(2,1)} %bitcast.8), calls=%async_computation.1 | async-start | bytes 2097152 | tf_op jit(solution)/shard_map/all_to_all | solution.py:52
  249.9 8.4 %all-to-all-start.6 = ((f32[4,1,128]{2,1,0:T(1,128)}), f32[4,1,128]{2,1,0:T(1,128)S(1)}, u32[]{:S(2)}, u32[]{:S(2)}) async-start(f32[4,1,128]{2,1,0:T(1,128)} %bitcast.17), calls=%async_computation.6 | async-start | bytes 4096 | tf_op jit(solution)/shard_map/all_to_all | solution.py:167
  258.3 7.8 %all-to-all-start.5 = ((f32[4,1,128]{2,1,0:T(1,128)}), f32[4,1,128]{2,1,0:T(1,128)S(1)}, u32[]{:S(2)}, u32[]{:S(2)}) async-start(f32[4,1,128]{2,1,0:T(1,128)} %bitcast.14), calls=%async_computation.5 | async-start | bytes 4096 | tf_op jit(solution)/shard_map/all_to_all | solution.py:164
  266.0 22.9 %all-to-all-start.4 = ((f32[4,128,1024]{2,1,0:T(8,128)}), f32[4,128,1024]{2,1,0:T(8,128)S(1)}, u32[]{:S(2)}, u32[]{:S(2)}) async-start(f32[4,128,1024]{2,1,0:T(8,128)} %bitcast.114), calls=%async_computation.4 | async-start | bytes 4194304 | tf_op jit(solution)/shard_map/all_to_all | solution.py:157
Sparse Core Ops, SparseCore 0:
  34.1 81.8 all-gather.2
where the time goes:
time: 299 us; the launch traced here: 298 us
  blocking collectives  95.9 us (32%)
  matrix products  71 us (24%)
  waiting for transfers between devices  64.5 us (22%)
  starting transfers between devices  18.2 us (6%)
  other arithmetic  17.5 us (6%)
  local copies, waits for them, and re-layouts  16 us (5%)
  between operations  14.2 us (5%)
    all_gather x1, waiting for transfers between devices, on_device(): part_rows = lax.all_gather(tgt_slots, 'blk', axis=0, tiled=True)  43.4 us
    dot_general x16, matrix products, tile_weight(): lax.dot_general(src_slots, rows_block, (((1,), (1,)), ((), ())), preferre...  39.5 us
    psum x1, blocking collectives, on_device(): summed_total, summed_weighted = lax.psum((part_total, part_sum), 'blk')  26.3 us
    unnamed x1, blocking collectives  25.9 us
    all_to_all x1, blocking collectives, on_device(): lax.all_to_all(tgt_pack, 'pair', split_axis=0, concat_axis=0, tiled=True)  19.2 us
    dot_general x8, matrix products, first_inner_step(): jnp.dot(weight.astype(jnp.bfloat16), rows_block, preferred_element_type=j...  18.4 us
    all_gather x1, blocking collectives, on_device(): part_live = lax.all_gather(move_live, 'blk', axis=0, tiled=True)  16 us
    all_to_all x1, waiting for transfers between devices, on_device(): lax.all_to_all(partner.reshape(buckets, capacity, width), 'pair', split_a...  14.3 us
  transfers between devices with their start and end apart: 6, of which 4 were waited for; matrix products, arithmetic and copies ran while one was open for 5% of the time, Pallas kernels for 0%

commit v1 on v0

v1 whole, which is shorter than its diff:
```python
import functools

import jax
import jax.numpy as jnp
from jax import lax
from jax.experimental import pallas as pl
from jax.experimental.pallas import tpu as pltpu
from jax.sharding import PartitionSpec as P

sharpness = 12.0
chunks = 4
f32 = jnp.float32
bf16 = jnp.bfloat16


def normalize(row_block):
    values = row_block.astype(f32)
    square = jnp.mean(values * values, axis=-1, keepdims=True)
    return (values * lax.rsqrt(square + 1e-06)).astype(bf16)


def safe_ratio(numer, denom):
    return numer / jnp.where(denom > 0.0, denom, 1.0)


def iota(shape, axis):
    return lax.broadcasted_iota(jnp.int32, shape, axis)


def kernel(
    buckets, columns, cap,
    src_ref, tgt_ref, src_row, src_col, tgt_row, tgt_col,
    out_ref, src_out, tgt_out,
    raw, slots, picks, packed, every, src_send, src_have, count_send, count_have,
    scores, weights, fwd_total, fwd_sum, back_sum, bwd_have, fore_have,
    part_send, part_have, smar_send, smar_have, tmar_send, tmar_have,
    up_sem, down_sem, block_sem, slot_ssem, slot_rsem, xs_sem, xr_sem, cs_sem, cr_sem,
    ss_sem, sr_sem, ns_sem, nr_sem, bs_sem, br_sem, fs_sem, fr_sem,
    ps_sem, pr_sem, ms_sem, mr_sem, ts_sem, tr_sem,
):
    rows, width = src_ref.shape
    line = columns // 2
    units = line // 2
    piece = width // chunks
    slot_total = buckets * cap
    me = lax.axis_index("pair")
    col = lax.axis_index("blk")
    z = col // 2
    core = col % 2
    other = z * 2 + (1 - core)

    def remote(src, dst, ssem, rsem, dev):
        return pltpu.make_async_remote_copy(
            src_ref=src, dst_ref=dst, send_sem=ssem, recv_sem=rsem,
            device_id=dev, device_id_type=pl.DeviceIdType.MESH,
        )

    barrier = pltpu.get_barrier_semaphore()
    for d in range(1, columns):
        pl.semaphore_signal(
            barrier, inc=1, device_id=(me, (col + d) % columns),
            device_id_type=pl.DeviceIdType.MESH,
        )
    for d in range(1, buckets):
        pl.semaphore_signal(
            barrier, inc=1, device_id=((me + d) % buckets, col),
            device_id_type=pl.DeviceIdType.MESH,
        )

    tgt_norm = normalize(tgt_ref[...])
    for h in range(chunks):
        raw[z, h] = tgt_norm[:, h * piece:(h + 1) * piece]

    def rank_row(lab_row, lab_col):
        same = (lab_col == lab_row) & (iota((rows, rows), 0) < iota((rows, rows), 1))
        return jnp.sum(same.astype(f32), axis=0, keepdims=True).astype(jnp.int32)

    tgt_rank = rank_row(tgt_row[...], tgt_col[...])
    tgt_slot = tgt_row[...] * cap + jnp.where(z < units, tgt_rank, cap - 1 - tgt_rank)
    slots[z] = jnp.broadcast_to(tgt_slot, (8, rows))
    pl.semaphore_wait(barrier, columns - 1 + buckets - 1)

    def slot_copy(d):
        return remote(
            slots.at[z], slots.at[z], slot_ssem.at[d], slot_rsem.at[z],
            (me, ((z + d) % line) * 2 + core),
        )

    for d in range(1, line):
        slot_copy(d).start()

    def up_copy(block, h):
        return remote(
            raw.at[block, h], raw.at[block, h], up_sem.at[block, h],
            block_sem.at[block, h], (me, jnp.minimum(z + 1, line - 1) * 2 + core),
        )

    def down_copy(block, h):
        return remote(
            raw.at[block, h], raw.at[block, h], down_sem.at[block, h],
            block_sem.at[block, h], (me, jnp.maximum(z - 1, 0) * 2 + core),
        )

    def send_own(h):
        @pl.when(z + 1 < line)
        def _():
            up_copy(z, h).start()

        @pl.when(z > 0)
        def _():
            down_copy(z, h).start()

    send_own(0)

    src_norm = normalize(src_ref[...])
    src_rank = rank_row(src_row[...], src_col[...])
    src_slot = src_row[...] * cap + src_rank
    src_pick = (iota((slot_total, rows), 0) == src_slot).astype(bf16)
    src_pack = jnp.dot(src_pick, src_norm, preferred_element_type=f32).astype(bf16)
    for b in range(buckets):
        src_send[b] = src_pack[b * cap:(b + 1) * cap]
        count = jnp.sum((src_row[...] == b).astype(f32), axis=1, keepdims=True)
        count_send[b] = jnp.broadcast_to(count, (8, 128))

    def src_copy(d):
        b = (me + d) % buckets
        return remote(src_send.at[b], src_have.at[me], ss_sem.at[d], sr_sem.at[d], (b, col))

    def count_copy(d):
        b = (me + d) % buckets
        return remote(count_send.at[b], count_have.at[me], ns_sem.at[d], nr_sem.at[d], (b, col))

    for d in range(1, buckets):
        src_copy(d).start()
        count_copy(d).start()
    src_have[me] = src_send[me]
    count_have[me] = count_send[me]

    def landed(ref, sem):
        remote(ref, ref, sem, sem, (me, other)).wait_recv()

    for d in range(1, line):
        block = (z + d) % line
        landed(slots.at[block], slot_rsem.at[block])
    for block in range(line):
        picks[block] = (iota((slot_total, rows), 0) == slots[block][0:1, :]).astype(bf16)

    def x_copy(h, u, d):
        b = (me + d) % buckets
        return remote(
            packed.at[h, u, b], every.at[h, core, u, me],
            xs_sem.at[h, u, d], xr_sem.at[h, u, d], (b, col),
        )

    def core_copy(h):
        return remote(
            every.at[h, core], every.at[h, core], cs_sem.at[h], cr_sem.at[h], (me, other)
        )

    def gather_blocks(h):
        if h + 1 < chunks:
            send_own(h + 1)
        for s in range(1, line):
            @pl.when(z - s >= 0)
            def _():
                block = jnp.maximum(z - s, 0)
                landed(raw.at[block, h], block_sem.at[block, h])

                @pl.when(z + 1 < line)
                def _():
                    up_copy(block, h).start()

            @pl.when(z + s < line)
            def _():
                block = jnp.minimum(z + s, line - 1)
                landed(raw.at[block, h], block_sem.at[block, h])

                @pl.when(z > 0)
                def _():
                    down_copy(block, h).start()
        for u in range(units):
            block = jnp.dot(picks[u], raw[u, h], preferred_element_type=f32) + jnp.dot(
                picks[u + units], raw[u + units, h], preferred_element_type=f32
            )
            packed[h, u] = block.astype(bf16).reshape(buckets, cap, piece)
            for d in range(1, buckets):
                x_copy(h, u, d).start()
            every[h, core, u, me] = packed[h, u, me]

    def pass_to_core(h):
        for u in range(units):
            for d in range(1, buckets):
                landed(every.at[h, core, u, (me - d + buckets) % buckets], xr_sem.at[h, u, d])
        core_copy(h).start()

    def add_scores(h):
        src_part = src_have[:, :, h * piece:(h + 1) * piece].reshape(slot_total, piece)

        def one(cu, _):
            block = every[h, cu // units, cu % units].reshape(slot_total, piece)
            term = lax.dot_general(
                src_part, block, (((1,), (1,)), ((), ())), preferred_element_type=f32
            )
            if h == 0:
                scores[cu] = term
            else:
                scores[cu] += term
            return 0

        lax.fori_loop(0, 2 * units, one, 0)

    for step in range(chunks + 2):
        if step < chunks:
            gather_blocks(step)
        if 1 <= step <= chunks:
            pass_to_core(step - 1)
        if step == 2:
            for d in range(1, buckets):
                landed(src_have.at[(me - d + buckets) % buckets], sr_sem.at[d])
                landed(count_have.at[(me - d + buckets) % buckets], nr_sem.at[d])
        if step >= 2:
            landed(every.at[step - 2, 1 - core], cr_sem.at[step - 2])
            add_scores(step - 2)

    fwd_total[...] = jnp.zeros_like(fwd_total)
    fwd_sum[...] = jnp.zeros_like(fwd_sum)
    zero_row = jnp.zeros((1, slot_total), f32)
    for cu in range(2 * units):
        def weigh(rb, state):
            tot, wsum = state
            at = pl.ds(pl.multiple_of(rb * cap, cap), cap)
            live = (iota((cap, 128), 0).astype(f32) < count_have[rb][0:1, :]).astype(f32)[:, 0:1]
            similar = scores[cu, at, :] * (1.0 / width)
            weight = jnp.exp(sharpness * similar) * live
            weighted = weight * similar
            scores[cu, at, :] = weight
            weights[cu, at, :] = weight.astype(bf16)
            fwd_total[at, :] += jnp.sum(weight, axis=1, keepdims=True)
            fwd_sum[at, :] += jnp.sum(weighted, axis=1, keepdims=True)
            return (
                tot + jnp.sum(weight, axis=0, keepdims=True),
                wsum + jnp.sum(weighted, axis=0, keepdims=True),
            )

        tot, wsum = lax.fori_loop(0, buckets, weigh, (zero_row, zero_row))
        bwd_have[col, cu:cu + 1, :] = tot
        bwd_have[col, 2 * units + cu:2 * units + cu + 1, :] = wsum

    def bwd_copy(d):
        return remote(
            bwd_have.at[col], bwd_have.at[col], bs_sem.at[d], br_sem.at[d],
            (me, (col + d) % columns),
        )

    def fore_copy(d):
        return remote(
            fore_have.at[col], fore_have.at[col], fs_sem.at[d], fr_sem.at[d],
            (me, (col + d) % columns),
        )

    for d in range(1, columns):
        bwd_copy(d).start()

    def part_copy(h, d):
        b = (me + d) % buckets
        return remote(
            part_send.at[h, b], part_have.at[h, me], ps_sem.at[h, d], pr_sem.at[h, d], (b, col)
        )

    scale = safe_ratio(1.0, fwd_total[...])

    def partner(h):
        acc = jnp.zeros((slot_total, piece), f32)
        for cu in range(2 * units):
            acc = acc + jnp.dot(
                weights[cu],
                every[h, cu // units, cu % units].reshape(slot_total, piece),
                preferred_element_type=f32,
            )
        part_send[h] = (acc * scale).astype(bf16).reshape(buckets, cap, piece)
        for d in range(1, buckets):
            part_copy(h, d).start()
        part_have[h, me] = part_send[h, me]

    for h in range(chunks):
        partner(h)

    for d in range(1, columns):
        landed(bwd_have.at[(col - d + columns) % columns], br_sem.at[d])
    bwd_all = bwd_have[0]
    for c in range(1, columns):
        bwd_all = bwd_all + bwd_have[c]
    bwd_total = bwd_all[:2 * units]
    bwd_stat = safe_ratio(bwd_all[2 * units:], bwd_total)
    back_sum[...] = jnp.zeros_like(back_sum)
    fore_have[col] = jnp.zeros(fore_have.shape[1:], f32)
    for cu in range(2 * units):
        stat_row = bwd_stat[cu:cu + 1, :]

        def margin(rb, fore):
            at = pl.ds(pl.multiple_of(rb * cap, cap), cap)
            weight = scores[cu, at, :]
            back_sum[at, :] += jnp.sum(weight * stat_row, axis=1, keepdims=True)
            stat = safe_ratio(fwd_sum[at, :], fwd_total[at, :])
            return fore + jnp.sum(weight * stat, axis=0, keepdims=True)

        fore_have[col, cu:cu + 1, :] = lax.fori_loop(0, buckets, margin, zero_row)
    for d in range(1, columns):
        fore_copy(d).start()

    fwd_stat = safe_ratio(fwd_sum[...], fwd_total[...])
    src_margin = fwd_stat - 0.5 * (fwd_stat + safe_ratio(back_sum[...], fwd_total[...]))
    eye = (iota((cap, 128), 0) == iota((cap, 128), 1)).astype(f32)
    for b in range(buckets):
        line_row = jnp.sum(src_margin[b * cap:(b + 1) * cap] * eye, axis=0, keepdims=True)
        smar_send[b] = jnp.broadcast_to(line_row, (8, 128))

    def smar_copy(d):
        b = (me + d) % buckets
        return remote(smar_send.at[b], smar_have.at[me], ms_sem.at[d], mr_sem.at[d], (b, col))

    for d in range(1, buckets):
        smar_copy(d).start()
    smar_have[me] = smar_send[me]

    for d in range(1, columns):
        landed(fore_have.at[(col - d + columns) % columns], fr_sem.at[d])
    fore_all = fore_have[0]
    for c in range(1, columns):
        fore_all = fore_all + fore_have[c]
    tgt_margin = bwd_stat - 0.5 * (bwd_stat + safe_ratio(fore_all[:2 * units], bwd_total))
    tmar_send[...] = jnp.zeros_like(tmar_send)
    for cu in range(2 * units):
        for b in range(buckets):
            tmar_send[cu, b, 0:1, 0:cap] = tgt_margin[cu:cu + 1, b * cap:(b + 1) * cap]
    mine = core * units + z % units

    def tmar_copy(d):
        b = (me + d) % buckets
        return remote(
            tmar_send.at[mine, b], tmar_have.at[me], ts_sem.at[d], tr_sem.at[d], (b, col)
        )

    for d in range(1, buckets):
        tmar_copy(d).start()
    tmar_have[me] = tmar_send[mine, me]

    lanes = iota((rows, rows), 0) > iota((rows, rows), 1)
    same = (src_col[...] == src_row[...]) & lanes
    rank_col = jnp.sum(same.astype(f32), axis=1, keepdims=True).astype(jnp.int32)
    unpick = (iota((rows, slot_total), 1) == src_col[...] * cap + rank_col).astype(bf16)
    for h in range(chunks):
        for d in range(1, buckets):
            landed(part_have.at[h, (me - d + buckets) % buckets], pr_sem.at[h, d])
        out_ref[:, h * piece:(h + 1) * piece] = jnp.dot(
            unpick, part_have[h].reshape(slot_total, piece), preferred_element_type=f32
        )
    for d in range(1, buckets):
        landed(smar_have.at[(me - d + buckets) % buckets], mr_sem.at[d])
        landed(tmar_have.at[(me - d + buckets) % buckets], tr_sem.at[d])

    def spread(have, slot):
        total = jnp.zeros((8, rows), f32)
        for b in range(buckets):
            spot = iota((128, rows), 0)
            pick = ((spot + b * cap == slot) & (spot < cap)).astype(f32)
            total = total + jnp.dot(
                have[b], pick, preferred_element_type=f32, precision=lax.Precision.HIGHEST
            )
        return total[0:1]

    src_out[...] = spread(smar_have, src_slot)
    tgt_out[...] = spread(tmar_have, tgt_slot)

    for d in range(1, line):
        slot_copy(d).wait_send()
    for h in range(chunks):
        for block in range(line):
            @pl.when((block <= z) & (z + 1 < line))
            def _():
                up_copy(block, h).wait_send()

            @pl.when((block >= z) & (z > 0))
            def _():
                down_copy(block, h).wait_send()
        core_copy(h).wait_send()
        for d in range(1, buckets):
            part_copy(h, d).wait_send()
            for u in range(units):
                x_copy(h, u, d).wait_send()
    for d in range(1, buckets):
        src_copy(d).wait_send()
        count_copy(d).wait_send()
        smar_copy(d).wait_send()
        tmar_copy(d).wait_send()
    for d in range(1, columns):
        bwd_copy(d).wait_send()
        fore_copy(d).wait_send()


def on_device(source, source_label, target, target_label):
    rows, width = source.shape
    buckets = lax.axis_size("pair")
    columns = lax.axis_size("blk")
    cap = 2 * rows // buckets
    slot_total = buckets * cap
    line = columns // 2
    units = line // 2
    piece = width // chunks
    fore_rows = max(8, 2 * units)
    vmem = pltpu.VMEM
    dma = pltpu.SemaphoreType.DMA
    scratch = [
        vmem((line, chunks, rows, piece), bf16),
        vmem((line, 8, rows), jnp.int32),
        vmem((line, slot_total, rows), bf16),
        vmem((chunks, units, buckets, cap, piece), bf16),
        vmem((chunks, 2, units, buckets, cap, piece), bf16),
        vmem((buckets, cap, width), bf16),
        vmem((buckets, cap, width), bf16),
        vmem((buckets, 8, 128), f32),
        vmem((buckets, 8, 128), f32),
        vmem((2 * units, slot_total, slot_total), f32),
        vmem((2 * units, slot_total, slot_total), bf16),
        vmem((slot_total, 1), f32),
        vmem((slot_total, 1), f32),
        vmem((slot_total, 1), f32),
        vmem((columns, 4 * units, slot_total), f32),
        vmem((columns, fore_rows, slot_total), f32),
        vmem((chunks, buckets, cap, piece), bf16),
        vmem((chunks, buckets, cap, piece), bf16),
        vmem((buckets, 8, 128), f32),
        vmem((buckets, 8, 128), f32),
        vmem((2 * units, buckets, 8, 128), f32),
        vmem((buckets, 8, 128), f32),
        dma((line, chunks)),
        dma((line, chunks)),
        dma((line, chunks)),
        dma((line,)),
        dma((line,)),
        dma((chunks, units, buckets)),
        dma((chunks, units, buckets)),
        dma((chunks,)),
        dma((chunks,)),
        dma((buckets,)),
        dma((buckets,)),
        dma((buckets,)),
        dma((buckets,)),
        dma((columns,)),
        dma((columns,)),
        dma((columns,)),
        dma((columns,)),
        dma((chunks, buckets)),
        dma((chunks, buckets)),
        dma((buckets,)),
        dma((buckets,)),
        dma((buckets,)),
        dma((buckets,)),
    ]
    partner, src_out, tgt_out = pl.pallas_call(
        functools.partial(kernel, buckets, columns, cap),
        out_shape=(
            jax.ShapeDtypeStruct((rows, width), f32),
            jax.ShapeDtypeStruct((1, rows), f32),
            jax.ShapeDtypeStruct((1, rows), f32),
        ),
        in_specs=[pl.BlockSpec(memory_space=pltpu.VMEM)] * 6,
        out_specs=(pl.BlockSpec(memory_space=pltpu.VMEM),) * 3,
        scratch_shapes=scratch,
        compiler_params=pltpu.CompilerParams(
            collective_id=0, has_side_effects=True, vmem_limit_bytes=56 * 1024 * 1024
        ),
        name="bitext",
    )(
        source,
        target,
        source_label.reshape(1, rows),
        source_label.reshape(rows, 1),
        target_label.reshape(1, rows),
        target_label.reshape(rows, 1),
    )
    return (partner, src_out.reshape(rows), tgt_out.reshape(rows))


def solution(mesh):
    return jax.shard_map(
        on_device,
        mesh=mesh,
        in_specs=(
            P(("pair", "blk"), None),
            P(("pair", "blk")),
            P(("pair", "blk"), None),
            P(("pair", "blk")),
        ),
        out_specs=(P(("pair", "blk"), None), P(("pair", "blk")), P(("pair", "blk"))),
        check_vma=False,
    )
```

time: 299 us -> 83.4 us (0.28)
  blocking collectives: 95.9 us -> 0 us
  Pallas kernels: 0 us -> 76.7 us
  matrix products: 71 us -> 0 us
  waiting for transfers between devices: 64.5 us -> 0 us
  starting transfers between devices: 18.2 us -> 0 us
  other arithmetic: 17.5 us -> 0 us
  between operations: 14.2 us -> 0.66 us
  local copies, waits for them, and re-layouts: 16 us -> 5.82 us
    pallas_call x0 -> x1, Pallas kernels: none -> 76.7 us  [on_device(): pl.pallas_call(functools.partial(kernel, buckets, columns, cap), out_shap...]
    dot_general x40 -> x0, matrix products: 71 us -> none  [the longest x16 39.5 us: tile_weight(): lax.dot_general(src_slots, rows_block, (((1,), (1,)), ((), ())), preferre...]
    all_gather x1 -> x0, waiting for transfers between devices: 43.4 us -> none  [on_device(): part_rows = lax.all_gather(tgt_slots, 'blk', axis=0, tiled=True)]
    all_to_all x2 -> x0, blocking collectives: 27.8 us -> none  [the longest x1 19.2 us: on_device(): lax.all_to_all(tgt_pack, 'pair', split_axis=0, concat_axis=0, tiled=True)]
    psum x1 -> x0, blocking collectives: 26.3 us -> none  [on_device(): summed_total, summed_weighted = lax.psum((part_total, part_sum), 'blk')]
    unnamed x1 -> x0, blocking collectives: 25.9 us -> none
    all_to_all x5 -> x0, waiting for transfers between devices: 21.1 us -> none  [the longest x1 14.3 us: on_device(): lax.all_to_all(partner.reshape(buckets, capacity, width), 'pair', split_a...]
    all_to_all x5 -> x0, starting transfers between devices: 18.2 us -> none  [the longest x1 4.25 us: on_device(): lax.all_to_all(src_pack, 'pair', split_axis=0, concat_axis=0, tiled=True)]
  transfers between devices with their start and end apart: 6 -> 0, of which waited for: 4 -> 0; matrix products, arithmetic and copies ran while one was open for 5% -> 0% of each run, Pallas kernels for 0% -> 0%
where the time goes in v1:
time: 83.4 us; the launch traced here: 83.2 us
  Pallas kernels  76.7 us (92%)
  local copies, waits for them, and re-layouts  5.82 us (7%)
    pallas_call x1, Pallas kernels, on_device(): pl.pallas_call(functools.partial(kernel, buckets, columns, cap), out_shap...  76.7 us
    unnamed x11, local copies, waits for them, and re-layouts  4.23 us

profile of v1, /device:TPU:0, one launch (start us, length us, event | category | flops | bytes accessed | tf_op | source)
XLA Modules:
  0.0 83.2 jit_solution(17780769089373885662)
XLA Ops:
  0.6 0.0 copy-start.1
  0.6 0.7 copy-done.1
  1.3 0.0 copy-start
  1.3 0.8 copy.8.tgt_col
  2.1 0.0 copy-done
  2.1 0.8 copy.7.src_col
  2.9 76.7 %bitext.1 = (f32[256,1024]{1,0:T(8,128)}, f32[1,256]{1,0:T(1,128)}, f32[1,256]{1,0:T(1,128)}) custom-call(bf16[256,1024]{1,0:T(8,128)(2,1)} %src_ref.1, bf16[256,1024]{1,0:T(8,128)(2,1)} %tgt_ref.1, s32[1,256]{1,0:T(1,128)} %bitcast.6, s32[256,1]{1,0:T(8,128)} %copy.7.src_col, s32[1,256]{1,0:T(1,128)} %bitcast.8, s32[256,1]{1,0:T(8,128)} %copy.8.tgt_col), custom_call_target="tpu_custom_call" | custom-call | tf_op jit(solution)/shard_map/bitext/pallas_call | solution.py:460
  79.6 0.0 copy-start.3
  79.7 2.3 %copy.12 = f32[256,1024]{1,0:T(8,128)} copy(f32[256,1024]{1,0:T(8,128)} %get-tuple-element.12) | data formatting | bytes 2097152
  82.0 0.0 copy-done.3
  82.0 0.0 copy-start.2
  82.0 0.6 copy.13
  82.5 0.1 copy-done.2
  82.6 0.6 copy.14
Async XLA Ops:
  0.6 0.7 copy-start.1
  1.3 0.8 copy-start
  79.6 2.3 %copy-start.3 = (f32[1,256]{1,0:T(1,128)S(1)}, f32[1,256]{1,0:T(1,128)}, u32[]{:S(2)}) copy-start(f32[1,256]{1,0:T(1,128)} %get-tuple-element.7) | copy-start | bytes 3076
  82.0 0.7 copy-start.2

commit v2 on v1

--- a/solution.py
+++ b/solution.py
@@ -27,13 +27,62 @@
     return lax.broadcasted_iota(jnp.int32, shape, axis)
 
 
+def to_column(row):
+    count = row.shape[1]
+    eye = iota((count, count), 0) == iota((count, count), 1)
+    return jnp.sum(jnp.where(eye, row.astype(f32), 0.0), axis=1, keepdims=True)
+
+
+def rank_row(lab_row):
+    count = lab_row.shape[1]
+    ahead = iota((count, count), 0) < iota((count, count), 1)
+    same = (to_column(lab_row) == lab_row.astype(f32)) & ahead
+    return jnp.sum(same.astype(f32), axis=0, keepdims=True).astype(jnp.int32)
+
+
+def target_slot(lab_row, cap, front):
+    rank = rank_row(lab_row)
+    return lab_row * cap + jnp.where(front, rank, cap - 1 - rank)
+
+
+def unpack_kernel(
+    buckets, columns, cap, src_row, tgt_row, part_have, smar_have, tmar_have,
+    out_ref, src_out, tgt_out,
+):
+    rows = src_row.shape[1]
+    slot_total = buckets * cap
+    piece = part_have.shape[-1]
+    front = lax.axis_index("blk") < columns // 2
+    src_slot = src_row[...] * cap + rank_row(src_row[...])
+    tgt_slot = target_slot(tgt_row[...], cap, front)
+    slot_col = to_column(src_slot).astype(jnp.int32)
+    unpick = (iota((rows, slot_total), 1) == slot_col).astype(bf16)
+    for h in range(chunks):
+        out_ref[:, h * piece:(h + 1) * piece] = jnp.dot(
+            unpick, part_have[h].reshape(slot_total, piece), preferred_element_type=f32
+        )
+
+    def spread(have, slot):
+        total = jnp.zeros((8, rows), f32)
+        for b in range(buckets):
+            spot = iota((128, rows), 0)
+            pick = ((spot + b * cap == slot) & (spot < cap)).astype(f32)
+            total = total + jnp.dot(
+                have[b], pick, preferred_element_type=f32, precision=lax.Precision.HIGHEST
+            )
+        return total[0:1]
+
+    src_out[...] = spread(smar_have, src_slot)
+    tgt_out[...] = spread(tmar_have, tgt_slot)
+
+
 def kernel(
     buckets, columns, cap,
-    src_ref, tgt_ref, src_row, src_col, tgt_row, tgt_col,
-    out_ref, src_out, tgt_out,
+    src_ref, tgt_ref, src_row, tgt_row,
+    part_have, smar_have, tmar_have,
     raw, slots, picks, packed, every, src_send, src_have, count_send, count_have,
     scores, weights, fwd_total, fwd_sum, back_sum, bwd_have, fore_have,
-    part_send, part_have, smar_send, smar_have, tmar_send, tmar_have,
+    part_send, smar_send, tmar_send,
     up_sem, down_sem, block_sem, slot_ssem, slot_rsem, xs_sem, xr_sem, cs_sem, cr_sem,
     ss_sem, sr_sem, ns_sem, nr_sem, bs_sem, br_sem, fs_sem, fr_sem,
     ps_sem, pr_sem, ms_sem, mr_sem, ts_sem, tr_sem,
@@ -71,12 +120,7 @@
     for h in range(chunks):
         raw[z, h] = tgt_norm[:, h * piece:(h + 1) * piece]
 
-    def rank_row(lab_row, lab_col):
-        same = (lab_col == lab_row) & (iota((rows, rows), 0) < iota((rows, rows), 1))
-        return jnp.sum(same.astype(f32), axis=0, keepdims=True).astype(jnp.int32)
-
-    tgt_rank = rank_row(tgt_row[...], tgt_col[...])
-    tgt_slot = tgt_row[...] * cap + jnp.where(z < units, tgt_rank, cap - 1 - tgt_rank)
+    tgt_slot = target_slot(tgt_row[...], cap, z < units)
     slots[z] = jnp.broadcast_to(tgt_slot, (8, rows))
     pl.semaphore_wait(barrier, columns - 1 + buckets - 1)
 
@@ -111,9 +155,10 @@
             down_copy(z, h).start()
 
     send_own(0)
+    send_own(1)
 
     src_norm = normalize(src_ref[...])
-    src_rank = rank_row(src_row[...], src_col[...])
+    src_rank = rank_row(src_row[...])
     src_slot = src_row[...] * cap + src_rank
     src_pick = (iota((slot_total, rows), 0) == src_slot).astype(bf16)
     src_pack = jnp.dot(src_pick, src_norm, preferred_element_type=f32).astype(bf16)
@@ -152,14 +197,36 @@
             xs_sem.at[h, u, d], xr_sem.at[h, u, d], (b, col),
         )
 
-    def core_copy(h):
-        return remote(
-            every.at[h, core], every.at[h, core], cs_sem.at[h], cr_sem.at[h], (me, other)
-        )
+    def core_copy(h, u):
+        return remote(
+            every.at[h, core, u], every.at[h, core, u], cs_sem.at[h, u], cr_sem.at[h, u],
+            (me, other),
+        )
+
+    def unit_at(t):
+        return jnp.where(z < units, t, units - 1 - t)
+
+    def pack_unit(h, u):
+        block = jnp.dot(picks[u], raw[u, h], preferred_element_type=f32) + jnp.dot(
+            picks[u + units], raw[u + units, h], preferred_element_type=f32
+        )
+        packed[h, u] = block.astype(bf16).reshape(buckets, cap, piece)
+        for d in range(1, buckets):
+            x_copy(h, u, d).start()
+        every[h, core, u, me] = packed[h, u, me]
+
+    def pack_ready(h, s):
+        lower = z < units
+        if s < line - 1 and s >= units:
+            u = jnp.where(lower, s - units, line - 1 - s)
+            pack_unit(h, u)
+        if s == line - 1:
+            for t in range(units - 1, units):
+                pack_unit(h, jnp.where(lower, t, units - 1 - t))
 
     def gather_blocks(h):
-        if h + 1 < chunks:
-            send_own(h + 1)
+        if h + 2 < chunks:
+            send_own(h + 2)
         for s in range(1, line):
             @pl.when(z - s >= 0)
             def _():
@@ -178,26 +245,29 @@
                 @pl.when(z > 0)
                 def _():
                     down_copy(block, h).start()
-        for u in range(units):
-            block = jnp.dot(picks[u], raw[u, h], preferred_element_type=f32) + jnp.dot(
-                picks[u + units], raw[u + units, h], preferred_element_type=f32
-            )
-            packed[h, u] = block.astype(bf16).reshape(buckets, cap, piece)
-            for d in range(1, buckets):
-                x_copy(h, u, d).start()
-            every[h, core, u, me] = packed[h, u, me]
+
+            pack_ready(h, s)
 
     def pass_to_core(h):
-        for u in range(units):
+        for t in range(units):
+            u = unit_at(t)
             for d in range(1, buckets):
                 landed(every.at[h, core, u, (me - d + buckets) % buckets], xr_sem.at[h, u, d])
-        core_copy(h).start()
+            core_copy(h, u).start()
 
     def add_scores(h):
         src_part = src_have[:, :, h * piece:(h + 1) * piece].reshape(slot_total, piece)
 
-        def one(cu, _):
-            block = every[h, cu // units, cu % units].reshape(slot_total, piece)
+        def one(t, _):
+            c = jnp.where(t < units, core, 1 - core)
+            u = unit_at(t % units)
+
+            @pl.when(t >= units)
+            def _():
+                landed(every.at[h, c, u], cr_sem.at[h, u])
+
+            cu = c * units + u
+            block = every[h, c, u].reshape(slot_total, piece)
             term = lax.dot_general(
                 src_part, block, (((1,), (1,)), ((), ())), preferred_element_type=f32
             )
@@ -219,32 +289,32 @@
                 landed(src_have.at[(me - d + buckets) % buckets], sr_sem.at[d])
                 landed(count_have.at[(me - d + buckets) % buckets], nr_sem.at[d])
         if step >= 2:
-            landed(every.at[step - 2, 1 - core], cr_sem.at[step - 2])
             add_scores(step - 2)
 
-    fwd_total[...] = jnp.zeros_like(fwd_total)
-    fwd_sum[...] = jnp.zeros_like(fwd_sum)
-    zero_row = jnp.zeros((1, slot_total), f32)
-    for cu in range(2 * units):
-        def weigh(rb, state):
-            tot, wsum = state
-            at = pl.ds(pl.multiple_of(rb * cap, cap), cap)
-            live = (iota((cap, 128), 0).astype(f32) < count_have[rb][0:1, :]).astype(f32)[:, 0:1]
+    bwd_have[col] = jnp.zeros(bwd_have.shape[1:], f32)
+
+    def block_of(b):
+        return pl.ds(pl.multiple_of(b * cap, cap), cap)
+
+    def weigh(b):
+        at = block_of(b)
+        live = (iota((cap, 128), 0).astype(f32) < count_have[b][0:1, :]).astype(f32)[:, 0:1]
+        total = jnp.zeros((cap, 1), f32)
+        wsum = jnp.zeros((cap, 1), f32)
+        for cu in range(2 * units):
             similar = scores[cu, at, :] * (1.0 / width)
             weight = jnp.exp(sharpness * similar) * live
             weighted = weight * similar
             scores[cu, at, :] = weight
             weights[cu, at, :] = weight.astype(bf16)
-            fwd_total[at, :] += jnp.sum(weight, axis=1, keepdims=True)
-            fwd_sum[at, :] += jnp.sum(weighted, axis=1, keepdims=True)
-            return (
-                tot + jnp.sum(weight, axis=0, keepdims=True),
-                wsum + jnp.sum(weighted, axis=0, keepdims=True),
+            total = total + jnp.sum(weight, axis=1, keepdims=True)
+            wsum = wsum + jnp.sum(weighted, axis=1, keepdims=True)
+            bwd_have[col, cu:cu + 1, :] += jnp.sum(weight, axis=0, keepdims=True)
+            bwd_have[col, 2 * units + cu:2 * units + cu + 1, :] += jnp.sum(
+                weighted, axis=0, keepdims=True
             )
-
-        tot, wsum = lax.fori_loop(0, buckets, weigh, (zero_row, zero_row))
-        bwd_have[col, cu:cu + 1, :] = tot
-        bwd_have[col, 2 * units + cu:2 * units + cu + 1, :] = wsum
+        fwd_total[at, :] = total
+        fwd_sum[at, :] = wsum
 
     def bwd_copy(d):
         return remote(
@@ -258,32 +328,40 @@
             (me, (col + d) % columns),
         )
 
+    def part_copy(h, d):
+        b = (me + d) % buckets
+        return remote(
+            part_send.at[h, b], part_have.at[h, me], ps_sem.at[h, d], pr_sem.at[h, d], (b, col)
+        )
+
+    def partner(d):
+        b = (me + d) % buckets
+        at = block_of(b)
+        scale = safe_ratio(1.0, fwd_total[at, :])
+        for h in range(chunks):
+            acc = jnp.zeros((cap, piece), f32)
+            for cu in range(2 * units):
+                acc = acc + jnp.dot(
+                    weights[cu, at, :],
+                    every[h, cu // units, cu % units].reshape(slot_total, piece),
+                    preferred_element_type=f32,
+                )
+            done = (acc * scale).astype(bf16)
+            if d == 0:
+                part_have[h, me] = done
+            else:
+                part_send[h, b] = done
+                part_copy(h, d).start()
+
+    weigh((me + 1) % buckets)
+    partner(1)
+    for d in range(2, buckets + 1):
+        weigh((me + d) % buckets)
     for d in range(1, columns):
         bwd_copy(d).start()
-
-    def part_copy(h, d):
-        b = (me + d) % buckets
-        return remote(
-            part_send.at[h, b], part_have.at[h, me], ps_sem.at[h, d], pr_sem.at[h, d], (b, col)
-        )
-
-    scale = safe_ratio(1.0, fwd_total[...])
-
-    def partner(h):
-        acc = jnp.zeros((slot_total, piece), f32)
-        for cu in range(2 * units):
-            acc = acc + jnp.dot(
-                weights[cu],
-                every[h, cu // units, cu % units].reshape(slot_total, piece),
-                preferred_element_type=f32,
-            )
-        part_send[h] = (acc * scale).astype(bf16).reshape(buckets, cap, piece)
-        for d in range(1, buckets):
-            part_copy(h, d).start()
-        part_have[h, me] = part_send[h, me]
-
-    for h in range(chunks):
-        partner(h)
+    for d in range(2, buckets):
+        partner(d)
+    partner(0)
 
     for d in range(1, columns):
         landed(bwd_have.at[(col - d + columns) % columns], br_sem.at[d])
@@ -293,6 +371,7 @@
     bwd_total = bwd_all[:2 * units]
     bwd_stat = safe_ratio(bwd_all[2 * units:], bwd_total)
     back_sum[...] = jnp.zeros_like(back_sum)
+    zero_row = jnp.zeros((1, slot_total), f32)
     fore_have[col] = jnp.zeros(fore_have.shape[1:], f32)
     for cu in range(2 * units):
         stat_row = bwd_stat[cu:cu + 1, :]
@@ -345,32 +424,12 @@
         tmar_copy(d).start()
     tmar_have[me] = tmar_send[mine, me]
 
-    lanes = iota((rows, rows), 0) > iota((rows, rows), 1)
-    same = (src_col[...] == src_row[...]) & lanes
-    rank_col = jnp.sum(same.astype(f32), axis=1, keepdims=True).astype(jnp.int32)
-    unpick = (iota((rows, slot_total), 1) == src_col[...] * cap + rank_col).astype(bf16)
-    for h in range(chunks):
-        for d in range(1, buckets):
-            landed(part_have.at[h, (me - d + buckets) % buckets], pr_sem.at[h, d])
-        out_ref[:, h * piece:(h + 1) * piece] = jnp.dot(
-            unpick, part_have[h].reshape(slot_total, piece), preferred_element_type=f32
-        )
     for d in range(1, buckets):
-        landed(smar_have.at[(me - d + buckets) % buckets], mr_sem.at[d])
-        landed(tmar_have.at[(me - d + buckets) % buckets], tr_sem.at[d])
-
-    def spread(have, slot):
-        total = jnp.zeros((8, rows), f32)
-        for b in range(buckets):
-            spot = iota((128, rows), 0)
-            pick = ((spot + b * cap == slot) & (spot < cap)).astype(f32)
-            total = total + jnp.dot(
-                have[b], pick, preferred_element_type=f32, precision=lax.Precision.HIGHEST
-            )
-        return total[0:1]
-
-    src_out[...] = spread(smar_have, src_slot)
-    tgt_out[...] = spread(tmar_have, tgt_slot)
+        b = (me - d + buckets) % buckets
+        for h in range(chunks):
+            landed(part_have.at[h, b], pr_sem.at[h, d])
+        landed(smar_have.at[b], mr_sem.at[d])
+        landed(tmar_have.at[b], tr_sem.at[d])
 
     for d in range(1, line):
         slot_copy(d).wait_send()
@@ -383,7 +442,8 @@
             @pl.when((block >= z) & (z > 0))
             def _():
                 down_copy(block, h).wait_send()
-        core_copy(h).wait_send()
+        for u in range(units):
+            core_copy(h, u).wait_send()
         for d in range(1, buckets):
             part_copy(h, d).wait_send()
             for u in range(units):
@@ -428,11 +488,8 @@
         vmem((columns, 4 * units, slot_total), f32),
         vmem((columns, fore_rows, slot_total), f32),
         vmem((chunks, buckets, cap, piece), bf16),
-        vmem((chunks, buckets, cap, piece), bf16),
-        vmem((buckets, 8, 128), f32),
         vmem((buckets, 8, 128), f32),
         vmem((2 * units, buckets, 8, 128), f32),
-        vmem((buckets, 8, 128), f32),
         dma((line, chunks)),
         dma((line, chunks)),
         dma((line, chunks)),
@@ -440,8 +497,8 @@
         dma((line,)),
         dma((chunks, units, buckets)),
         dma((chunks, units, buckets)),
-        dma((chunks,)),
-        dma((chunks,)),
+        dma((chunks, units)),
+        dma((chunks, units)),
         dma((buckets,)),
         dma((buckets,)),
         dma((buckets,)),
@@ -457,28 +514,35 @@
         dma((buckets,)),
         dma((buckets,)),
     ]
+    src_row = source_label.reshape(1, rows)
+    tgt_row = target_label.reshape(1, rows)
+    whole = pl.BlockSpec(memory_space=pltpu.VMEM)
+    part_have, smar_have, tmar_have = pl.pallas_call(
+        functools.partial(kernel, buckets, columns, cap),
+        out_shape=(
+            jax.ShapeDtypeStruct((chunks, buckets, cap, piece), bf16),
+            jax.ShapeDtypeStruct((buckets, 8, 128), f32),
+            jax.ShapeDtypeStruct((buckets, 8, 128), f32),
+        ),
+        in_specs=[whole] * 4,
+        out_specs=(whole,) * 3,
+        scratch_shapes=scratch,
+        compiler_params=pltpu.CompilerParams(
+            collective_id=0, has_side_effects=True, vmem_limit_bytes=56 * 1024 * 1024
+        ),
+        name="bitext",
+    )(source, target, src_row, tgt_row)
     partner, src_out, tgt_out = pl.pallas_call(
-        functools.partial(kernel, buckets, columns, cap),
+        functools.partial(unpack_kernel, buckets, columns, cap),
         out_shape=(
             jax.ShapeDtypeStruct((rows, width), f32),
             jax.ShapeDtypeStruct((1, rows), f32),
             jax.ShapeDtypeStruct((1, rows), f32),
         ),
-        in_specs=[pl.BlockSpec(memory_space=pltpu.VMEM)] * 6,
-        out_specs=(pl.BlockSpec(memory_space=pltpu.VMEM),) * 3,
-        scratch_shapes=scratch,
-        compiler_params=pltpu.CompilerParams(
-            collective_id=0, has_side_effects=True, vmem_limit_bytes=56 * 1024 * 1024
-        ),
-        name="bitext",
-    )(
-        source,
-        target,
-        source_label.reshape(1, rows),
-        source_label.reshape(rows, 1),
-        target_label.reshape(1, rows),
-        target_label.reshape(rows, 1),
-    )
+        in_specs=[whole] * 5,
+        out_specs=(whole,) * 3,
+        name="unpack",
+    )(src_row, tgt_row, part_have, smar_have, tmar_have)
     return (partner, src_out.reshape(rows), tgt_out.reshape(rows))
 
 

time: 83.4 us -> 77.6 us (0.930)
  local copies, waits for them, and re-layouts: 5.82 us -> 0 us
    unnamed x11 -> x0, local copies, waits for them, and re-layouts: 4.23 us -> none
    pallas_call x0 -> x1, Pallas kernels: none -> 2.94 us  [on_device(): pl.pallas_call(functools.partial(unpack_kernel, buckets, columns, cap), o...]
    pallas_call x1, Pallas kernels: 76.7 us -> 73.8 us  [on_device(): pl.pallas_call(functools.partial(kernel, buckets, columns, cap), out_shap...]
    reshape x2 -> x0, local copies, waits for them, and re-layouts: 1.59 us -> none  [the longest x1 0.8 us: on_device(): source_label.reshape(rows, 1)]
where the time goes in v2:
time: 77.6 us; the launch traced here: 77.4 us
  Pallas kernels  76.8 us (99%)
    pallas_call x1, Pallas kernels, on_device(): pl.pallas_call(functools.partial(kernel, buckets, columns, cap), out_shap...  73.8 us
    pallas_call x1, Pallas kernels, on_device(): pl.pallas_call(functools.partial(unpack_kernel, buckets, columns, cap), o...  2.94 us

profile of v2, /device:TPU:0, one launch (start us, length us, event | category | flops | bytes accessed | tf_op | source)
XLA Modules:
  0.0 77.4 jit_solution(8096224246912110676)
XLA Ops:
  0.6 73.8 %bitext.1 = (bf16[4,4,128,256]{3,2,1,0:T(8,128)(2,1)}, f32[4,8,128]{2,1,0:T(8,128)}, f32[4,8,128]{2,1,0:T(8,128)}) custom-call(bf16[256,1024]{1,0:T(8,128)(2,1)} %src_ref.1, bf16[256,1024]{1,0:T(8,128)(2,1)} %tgt_ref.1, s32[1,256]{1,0:T(1,128)} %bitcast.4, s32[1,256]{1,0:T(1,128)} %bitcast.6), custom_call_target="tpu_custom_call" | custom-call | tf_op jit(solution)/shard_map/bitext/pallas_call | solution.py:520
  74.5 2.9 %unpack.1 = (f32[256,1024]{1,0:T(8,128)}, f32[1,256]{1,0:T(1,128)}, f32[1,256]{1,0:T(1,128)}) custom-call(s32[1,256]{1,0:T(1,128)} %bitcast.5, s32[1,256]{1,0:T(1,128)} %bitcast.7, bf16[4,4,128,256]{3,2,1,0:T(8,128)(2,1)} %get-tuple-element.9.part_have, f32[4,8,128]{2,1,0:T(8,128)} %get-tuple-element.10.smar_have, f32[4,8,128]{2,1,0:T(8,128)} %get-tuple-element.11.tmar_have), custom_call_target="tpu_custom_call" | custom-call | tf_op jit(solution)/shard_map/unpack/pallas_call | solution.py:535

commit v3 on v2

--- a/solution.py
+++ b/solution.py
@@ -246,6 +246,10 @@
                 def _():
                     down_copy(block, h).start()
 
+            if s == 1:
+                between(h)
+            if s == 2 and h >= 2:
+                add_scores(h - 2, units, 2 * units)
             pack_ready(h, s)
 
     def pass_to_core(h):
@@ -255,7 +259,7 @@
                 landed(every.at[h, core, u, (me - d + buckets) % buckets], xr_sem.at[h, u, d])
             core_copy(h, u).start()
 
-    def add_scores(h):
+    def add_scores(h, first, last):
         src_part = src_have[:, :, h * piece:(h + 1) * piece].reshape(slot_total, piece)
 
         def one(t, _):
@@ -277,19 +281,24 @@
                 scores[cu] += term
             return 0
 
-        lax.fori_loop(0, 2 * units, one, 0)
-
-    for step in range(chunks + 2):
-        if step < chunks:
-            gather_blocks(step)
-        if 1 <= step <= chunks:
-            pass_to_core(step - 1)
-        if step == 2:
+        lax.fori_loop(first, last, one, 0)
+
+    def between(h):
+        if h >= 1:
+            pass_to_core(h - 1)
+        if h == 2:
             for d in range(1, buckets):
                 landed(src_have.at[(me - d + buckets) % buckets], sr_sem.at[d])
                 landed(count_have.at[(me - d + buckets) % buckets], nr_sem.at[d])
-        if step >= 2:
-            add_scores(step - 2)
+        if h >= 2:
+            add_scores(h - 2, 0, units)
+
+    for step in range(chunks):
+        gather_blocks(step)
+    add_scores(chunks - 2, 0, units)
+    pass_to_core(chunks - 1)
+    add_scores(chunks - 2, units, 2 * units)
+    add_scores(chunks - 1, 0, 2 * units)
 
     bwd_have[col] = jnp.zeros(bwd_have.shape[1:], f32)
 
@@ -302,8 +311,9 @@
         total = jnp.zeros((cap, 1), f32)
         wsum = jnp.zeros((cap, 1), f32)
         for cu in range(2 * units):
-            similar = scores[cu, at, :] * (1.0 / width)
-            weight = jnp.exp(sharpness * similar) * live
+            inner = scores[cu, at, :]
+            similar = inner * (1.0 / width)
+            weight = jnp.exp2(inner * (sharpness * 1.4426950408889634 / width)) * live
             weighted = weight * similar
             scores[cu, at, :] = weight
             weights[cu, at, :] = weight.astype(bf16)
@@ -334,34 +344,25 @@
             part_send.at[h, b], part_have.at[h, me], ps_sem.at[h, d], pr_sem.at[h, d], (b, col)
         )
 
-    def partner(d):
-        b = (me + d) % buckets
-        at = block_of(b)
-        scale = safe_ratio(1.0, fwd_total[at, :])
-        for h in range(chunks):
-            acc = jnp.zeros((cap, piece), f32)
-            for cu in range(2 * units):
-                acc = acc + jnp.dot(
-                    weights[cu, at, :],
-                    every[h, cu // units, cu % units].reshape(slot_total, piece),
-                    preferred_element_type=f32,
-                )
-            done = (acc * scale).astype(bf16)
-            if d == 0:
-                part_have[h, me] = done
-            else:
-                part_send[h, b] = done
-                part_copy(h, d).start()
-
-    weigh((me + 1) % buckets)
-    partner(1)
-    for d in range(2, buckets + 1):
-        weigh((me + d) % buckets)
+    def partner(h):
+        acc = jnp.zeros((slot_total, piece), f32)
+        for cu in range(2 * units):
+            acc = acc + jnp.dot(
+                weights[cu],
+                every[h, cu // units, cu % units].reshape(slot_total, piece),
+                preferred_element_type=f32,
+            )
+        part_send[h] = (acc * scale).astype(bf16).reshape(buckets, cap, piece)
+        for d in range(1, buckets):
+            part_copy(h, d).start()
+        part_have[h, me] = part_send[h, me]
+
+    lax.fori_loop(0, buckets, lambda b, _: (weigh(b), 0)[1], 0)
     for d in range(1, columns):
         bwd_copy(d).start()
-    for d in range(2, buckets):
-        partner(d)
-    partner(0)
+    scale = safe_ratio(1.0, fwd_total[...])
+    for h in range(chunks // 2):
+        partner(h)
 
     for d in range(1, columns):
         landed(bwd_have.at[(col - d + columns) % columns], br_sem.at[d])
@@ -386,6 +387,9 @@
         fore_have[col, cu:cu + 1, :] = lax.fori_loop(0, buckets, margin, zero_row)
     for d in range(1, columns):
         fore_copy(d).start()
+
+    for h in range(chunks // 2, chunks):
+        partner(h)
 
     fwd_stat = safe_ratio(fwd_sum[...], fwd_total[...])
     src_margin = fwd_stat - 0.5 * (fwd_stat + safe_ratio(back_sum[...], fwd_total[...]))

time: 77.6 us -> 82.1 us (1.058)
  Pallas kernels: 76.8 us -> 81.3 us
    pallas_call x1, Pallas kernels: 73.8 us -> 78.4 us  [on_device(): pl.pallas_call(functools.partial(kernel, buckets, columns, cap), out_shap...]
where the time goes in v3:
time: 82.1 us; the launch traced here: 82 us
  Pallas kernels  81.3 us (99%)
    pallas_call x1, Pallas kernels, on_device(): pl.pallas_call(functools.partial(kernel, buckets, columns, cap), out_shap...  78.4 us
    pallas_call x1, Pallas kernels, on_device(): pl.pallas_call(functools.partial(unpack_kernel, buckets, columns, cap), o...  2.94 us

profile of v3, /device:TPU:0, one launch (start us, length us, event | category | flops | bytes accessed | tf_op | source)
XLA Modules:
  0.0 82.0 jit_solution(2887586595483755530)
XLA Ops:
  0.6 78.4 %bitext.1 = (bf16[4,4,128,256]{3,2,1,0:T(8,128)(2,1)}, f32[4,8,128]{2,1,0:T(8,128)}, f32[4,8,128]{2,1,0:T(8,128)}) custom-call(bf16[256,1024]{1,0:T(8,128)(2,1)} %src_ref.1, bf16[256,1024]{1,0:T(8,128)(2,1)} %tgt_ref.1, s32[1,256]{1,0:T(1,128)} %bitcast.4, s32[1,256]{1,0:T(1,128)} %bitcast.6), custom_call_target="tpu_custom_call" | custom-call | tf_op jit(solution)/shard_map/bitext/pallas_call | solution.py:524
  79.0 2.9 %unpack.1 = (f32[256,1024]{1,0:T(8,128)}, f32[1,256]{1,0:T(1,128)}, f32[1,256]{1,0:T(1,128)}) custom-call(s32[1,256]{1,0:T(1,128)} %bitcast.5, s32[1,256]{1,0:T(1,128)} %bitcast.7, bf16[4,4,128,256]{3,2,1,0:T(8,128)(2,1)} %get-tuple-element.9.part_have, f32[4,8,128]{2,1,0:T(8,128)} %get-tuple-element.10.smar_have, f32[4,8,128]{2,1,0:T(8,128)} %get-tuple-element.11.tmar_have), custom_call_target="tpu_custom_call" | custom-call | tf_op jit(solution)/shard_map/unpack/pallas_call | solution.py:539

commit v4 on v3

--- a/solution.py
+++ b/solution.py
@@ -83,7 +83,7 @@
     raw, slots, picks, packed, every, src_send, src_have, count_send, count_have,
     scores, weights, fwd_total, fwd_sum, back_sum, bwd_have, fore_have,
     part_send, smar_send, tmar_send,
-    up_sem, down_sem, block_sem, slot_ssem, slot_rsem, xs_sem, xr_sem, cs_sem, cr_sem,
+    up_sem, down_sem, far_sem, block_sem, slot_ssem, slot_rsem, xs_sem, xr_sem, cs_sem, cr_sem,
     ss_sem, sr_sem, ns_sem, nr_sem, bs_sem, br_sem, fs_sem, fr_sem,
     ps_sem, pr_sem, ms_sem, mr_sem, ts_sem, tr_sem,
 ):
@@ -145,7 +145,27 @@
             block_sem.at[block, h], (me, jnp.maximum(z - 1, 0) * 2 + core),
         )
 
+    def up_far(h):
+        return remote(
+            raw.at[z, h], raw.at[z, h], far_sem.at[0, h],
+            block_sem.at[z, h], (me, jnp.minimum(z + 2, line - 1) * 2 + core),
+        )
+
+    def down_far(h):
+        return remote(
+            raw.at[z, h], raw.at[z, h], far_sem.at[1, h],
+            block_sem.at[z, h], (me, jnp.maximum(z - 2, 0) * 2 + core),
+        )
+
     def send_own(h):
+        @pl.when(z + 2 < line)
+        def _():
+            up_far(h).start()
+
+        @pl.when(z > 1)
+        def _():
+            down_far(h).start()
+
         @pl.when(z + 1 < line)
         def _():
             up_copy(z, h).start()
@@ -233,7 +253,7 @@
                 block = jnp.maximum(z - s, 0)
                 landed(raw.at[block, h], block_sem.at[block, h])
 
-                @pl.when(z + 1 < line)
+                @pl.when((z + 1 < line) & (s > 1))
                 def _():
                     up_copy(block, h).start()
 
@@ -242,14 +262,10 @@
                 block = jnp.minimum(z + s, line - 1)
                 landed(raw.at[block, h], block_sem.at[block, h])
 
-                @pl.when(z > 0)
+                @pl.when((z > 0) & (s > 1))
                 def _():
                     down_copy(block, h).start()
 
-            if s == 1:
-                between(h)
-            if s == 2 and h >= 2:
-                add_scores(h - 2, units, 2 * units)
             pack_ready(h, s)
 
     def pass_to_core(h):
@@ -283,22 +299,17 @@
 
         lax.fori_loop(first, last, one, 0)
 
-    def between(h):
-        if h >= 1:
-            pass_to_core(h - 1)
-        if h == 2:
+    for step in range(chunks + 2):
+        if step < chunks:
+            gather_blocks(step)
+        if 1 <= step <= chunks:
+            pass_to_core(step - 1)
+        if step == 2:
             for d in range(1, buckets):
                 landed(src_have.at[(me - d + buckets) % buckets], sr_sem.at[d])
                 landed(count_have.at[(me - d + buckets) % buckets], nr_sem.at[d])
-        if h >= 2:
-            add_scores(h - 2, 0, units)
-
-    for step in range(chunks):
-        gather_blocks(step)
-    add_scores(chunks - 2, 0, units)
-    pass_to_core(chunks - 1)
-    add_scores(chunks - 2, units, 2 * units)
-    add_scores(chunks - 1, 0, 2 * units)
+        if step >= 2:
+            add_scores(step - 2, 0, 2 * units)
 
     bwd_have[col] = jnp.zeros(bwd_have.shape[1:], f32)
 
@@ -439,13 +450,21 @@
         slot_copy(d).wait_send()
     for h in range(chunks):
         for block in range(line):
-            @pl.when((block <= z) & (z + 1 < line))
+            @pl.when((block <= z) & (block != z - 1) & (z + 1 < line))
             def _():
                 up_copy(block, h).wait_send()
 
-            @pl.when((block >= z) & (z > 0))
+            @pl.when((block >= z) & (block != z + 1) & (z > 0))
             def _():
                 down_copy(block, h).wait_send()
+        @pl.when(z + 2 < line)
+        def _():
+            up_far(h).wait_send()
+
+        @pl.when(z > 1)
+        def _():
+            down_far(h).wait_send()
+
         for u in range(units):
             core_copy(h, u).wait_send()
         for d in range(1, buckets):
@@ -496,6 +515,7 @@
         vmem((2 * units, buckets, 8, 128), f32),
         dma((line, chunks)),
         dma((line, chunks)),
+        dma((2, chunks)),
         dma((line, chunks)),
         dma((line,)),
         dma((line,)),

time: 82.1 us -> 81.6 us (level)
  no operation moved by 1% of the time
where the time goes in v4:
time: 81.6 us; the launch traced here: 81.4 us
  Pallas kernels  80.8 us (99%)
    pallas_call x1, Pallas kernels, on_device(): pl.pallas_call(functools.partial(kernel, buckets, columns, cap), out_shap...  77.8 us
    pallas_call x1, Pallas kernels, on_device(): pl.pallas_call(functools.partial(unpack_kernel, buckets, columns, cap), o...  2.94 us

profile of v4, /device:TPU:0, one launch (start us, length us, event | category | flops | bytes accessed | tf_op | source)
XLA Modules:
  0.0 81.4 jit_solution(10588497562746069603)
XLA Ops:
  0.6 77.8 %bitext.1 = (bf16[4,4,128,256]{3,2,1,0:T(8,128)(2,1)}, f32[4,8,128]{2,1,0:T(8,128)}, f32[4,8,128]{2,1,0:T(8,128)}) custom-call(bf16[256,1024]{1,0:T(8,128)(2,1)} %src_ref.1, bf16[256,1024]{1,0:T(8,128)(2,1)} %tgt_ref.1, s32[1,256]{1,0:T(1,128)} %bitcast.4, s32[1,256]{1,0:T(1,128)} %bitcast.6), custom_call_target="tpu_custom_call" | custom-call | tf_op jit(solution)/shard_map/bitext/pallas_call | solution.py:544
  78.5 2.9 %unpack.1 = (f32[256,1024]{1,0:T(8,128)}, f32[1,256]{1,0:T(1,128)}, f32[1,256]{1,0:T(1,128)}) custom-call(s32[1,256]{1,0:T(1,128)} %bitcast.5, s32[1,256]{1,0:T(1,128)} %bitcast.7, bf16[4,4,128,256]{3,2,1,0:T(8,128)(2,1)} %get-tuple-element.9.part_have, f32[4,8,128]{2,1,0:T(8,128)} %get-tuple-element.10.smar_have, f32[4,8,128]{2,1,0:T(8,128)} %get-tuple-element.11.tmar_have), custom_call_target="tpu_custom_call" | custom-call | tf_op jit(solution)/shard_map/unpack/pallas_call | solution.py:559

commit v5 on v4

--- a/solution.py
+++ b/solution.py
@@ -355,25 +355,33 @@
             part_send.at[h, b], part_have.at[h, me], ps_sem.at[h, d], pr_sem.at[h, d], (b, col)
         )
 
-    def partner(h):
-        acc = jnp.zeros((slot_total, piece), f32)
-        for cu in range(2 * units):
-            acc = acc + jnp.dot(
-                weights[cu],
-                every[h, cu // units, cu % units].reshape(slot_total, piece),
-                preferred_element_type=f32,
-            )
-        part_send[h] = (acc * scale).astype(bf16).reshape(buckets, cap, piece)
-        for d in range(1, buckets):
-            part_copy(h, d).start()
-        part_have[h, me] = part_send[h, me]
-
-    lax.fori_loop(0, buckets, lambda b, _: (weigh(b), 0)[1], 0)
+    def partner(d):
+        b = (me + d) % buckets
+        at = block_of(b)
+        scale = safe_ratio(1.0, fwd_total[at, :])
+        for h in range(chunks):
+            acc = jnp.zeros((cap, piece), f32)
+            for cu in range(2 * units):
+                acc = acc + jnp.dot(
+                    weights[cu, at, :],
+                    every[h, cu // units, cu % units].reshape(slot_total, piece),
+                    preferred_element_type=f32,
+                )
+            done = (acc * scale).astype(bf16)
+            if d == 0:
+                part_have[h, me] = done
+            else:
+                part_send[h, b] = done
+                part_copy(h, d).start()
+
+    weigh((me + 1) % buckets)
+    partner(1)
+    for d in range(2, buckets + 1):
+        weigh((me + d) % buckets)
     for d in range(1, columns):
         bwd_copy(d).start()
-    scale = safe_ratio(1.0, fwd_total[...])
-    for h in range(chunks // 2):
-        partner(h)
+    for d in range(2, buckets - 1):
+        partner(d)
 
     for d in range(1, columns):
         landed(bwd_have.at[(col - d + columns) % columns], br_sem.at[d])
@@ -399,8 +407,7 @@
     for d in range(1, columns):
         fore_copy(d).start()
 
-    for h in range(chunks // 2, chunks):
-        partner(h)
+    partner(buckets - 1)
 
     fwd_stat = safe_ratio(fwd_sum[...], fwd_total[...])
     src_margin = fwd_stat - 0.5 * (fwd_stat + safe_ratio(back_sum[...], fwd_total[...]))
@@ -417,6 +424,7 @@
         smar_copy(d).start()
     smar_have[me] = smar_send[me]
 
+    partner(0)
     for d in range(1, columns):
         landed(fore_have.at[(col - d + columns) % columns], fr_sem.at[d])
     fore_all = fore_have[0]

time: 81.6 us -> 82 us (level)
  no operation moved by 1% of the time
where the time goes in v5:
time: 82 us; the launch traced here: 81.8 us
  Pallas kernels  81.2 us (99%)
    pallas_call x1, Pallas kernels, on_device(): pl.pallas_call(functools.partial(kernel, buckets, columns, cap), out_shap...  78.2 us
    pallas_call x1, Pallas kernels, on_device(): pl.pallas_call(functools.partial(unpack_kernel, buckets, columns, cap), o...  2.94 us

profile of v5, /device:TPU:0, one launch (start us, length us, event | category | flops | bytes accessed | tf_op | source)
XLA Modules:
  0.0 81.8 jit_solution(13865442809162961624)
XLA Ops:
  0.6 78.2 %bitext.1 = (bf16[4,4,128,256]{3,2,1,0:T(8,128)(2,1)}, f32[4,8,128]{2,1,0:T(8,128)}, f32[4,8,128]{2,1,0:T(8,128)}) custom-call(bf16[256,1024]{1,0:T(8,128)(2,1)} %src_ref.1, bf16[256,1024]{1,0:T(8,128)(2,1)} %tgt_ref.1, s32[1,256]{1,0:T(1,128)} %bitcast.4, s32[1,256]{1,0:T(1,128)} %bitcast.6), custom_call_target="tpu_custom_call" | custom-call | tf_op jit(solution)/shard_map/bitext/pallas_call | solution.py:552
  78.9 2.9 %unpack.1 = (f32[256,1024]{1,0:T(8,128)}, f32[1,256]{1,0:T(1,128)}, f32[1,256]{1,0:T(1,128)}) custom-call(s32[1,256]{1,0:T(1,128)} %bitcast.5, s32[1,256]{1,0:T(1,128)} %bitcast.7, bf16[4,4,128,256]{3,2,1,0:T(8,128)(2,1)} %get-tuple-element.9.part_have, f32[4,8,128]{2,1,0:T(8,128)} %get-tuple-element.10.smar_have, f32[4,8,128]{2,1,0:T(8,128)} %get-tuple-element.11.tmar_have), custom_call_target="tpu_custom_call" | custom-call | tf_op jit(solution)/shard_map/unpack/pallas_call | solution.py:567

commit v6 on v2

--- a/solution.py
+++ b/solution.py
@@ -126,7 +126,7 @@
 
     def slot_copy(d):
         return remote(
-            slots.at[z], slots.at[z], slot_ssem.at[d], slot_rsem.at[z],
+            slots.at[z], slots.at[z], slot_ssem.at[0], slot_rsem.at[0],
             (me, ((z + d) % line) * 2 + core),
         )
 
@@ -135,13 +135,13 @@
 
     def up_copy(block, h):
         return remote(
-            raw.at[block, h], raw.at[block, h], up_sem.at[block, h],
+            raw.at[block, h], raw.at[block, h], up_sem.at[block],
             block_sem.at[block, h], (me, jnp.minimum(z + 1, line - 1) * 2 + core),
         )
 
     def down_copy(block, h):
         return remote(
-            raw.at[block, h], raw.at[block, h], down_sem.at[block, h],
+            raw.at[block, h], raw.at[block, h], down_sem.at[block],
             block_sem.at[block, h], (me, jnp.maximum(z - 1, 0) * 2 + core),
         )
 
@@ -169,11 +169,11 @@
 
     def src_copy(d):
         b = (me + d) % buckets
-        return remote(src_send.at[b], src_have.at[me], ss_sem.at[d], sr_sem.at[d], (b, col))
+        return remote(src_send.at[b], src_have.at[me], ss_sem.at[0], sr_sem.at[0], (b, col))
 
     def count_copy(d):
         b = (me + d) % buckets
-        return remote(count_send.at[b], count_have.at[me], ns_sem.at[d], nr_sem.at[d], (b, col))
+        return remote(count_send.at[b], count_have.at[me], ns_sem.at[0], nr_sem.at[0], (b, col))
 
     for d in range(1, buckets):
         src_copy(d).start()
@@ -184,9 +184,7 @@
     def landed(ref, sem):
         remote(ref, ref, sem, sem, (me, other)).wait_recv()
 
-    for d in range(1, line):
-        block = (z + d) % line
-        landed(slots.at[block], slot_rsem.at[block])
+    landed(slots.at[pl.ds(0, line - 1)], slot_rsem.at[0])
     for block in range(line):
         picks[block] = (iota((slot_total, rows), 0) == slots[block][0:1, :]).astype(bf16)
 
@@ -194,12 +192,12 @@
         b = (me + d) % buckets
         return remote(
             packed.at[h, u, b], every.at[h, core, u, me],
-            xs_sem.at[h, u, d], xr_sem.at[h, u, d], (b, col),
+            xs_sem.at[0], xr_sem.at[h, u], (b, col),
         )
 
     def core_copy(h, u):
         return remote(
-            every.at[h, core, u], every.at[h, core, u], cs_sem.at[h, u], cr_sem.at[h, u],
+            every.at[h, core, u], every.at[h, core, u], cs_sem.at[0], cr_sem.at[h, u],
             (me, other),
         )
 
@@ -225,8 +223,10 @@
                 pack_unit(h, jnp.where(lower, t, units - 1 - t))
 
     def gather_blocks(h):
-        if h + 2 < chunks:
+        @pl.when(h + 2 < chunks)
+        def _():
             send_own(h + 2)
+
         for s in range(1, line):
             @pl.when(z - s >= 0)
             def _():
@@ -251,12 +251,11 @@
     def pass_to_core(h):
         for t in range(units):
             u = unit_at(t)
-            for d in range(1, buckets):
-                landed(every.at[h, core, u, (me - d + buckets) % buckets], xr_sem.at[h, u, d])
+            landed(every.at[h, core, u, pl.ds(0, buckets - 1)], xr_sem.at[h, u])
             core_copy(h, u).start()
 
     def add_scores(h):
-        src_part = src_have[:, :, h * piece:(h + 1) * piece].reshape(slot_total, piece)
+        src_part = src_have[:, :, pl.ds(pl.multiple_of(h * piece, piece), piece)].reshape(slot_total, piece)
 
         def one(t, _):
             c = jnp.where(t < units, core, 1 - core)
@@ -271,25 +270,39 @@
             term = lax.dot_general(
                 src_part, block, (((1,), (1,)), ((), ())), preferred_element_type=f32
             )
-            if h == 0:
+            @pl.when(h == 0)
+            def _():
                 scores[cu] = term
-            else:
+
+            @pl.when(h > 0)
+            def _():
                 scores[cu] += term
+
             return 0
 
         lax.fori_loop(0, 2 * units, one, 0)
 
-    for step in range(chunks + 2):
-        if step < chunks:
+    def one_step(step, _):
+        @pl.when(step < chunks)
+        def _():
             gather_blocks(step)
-        if 1 <= step <= chunks:
+
+        @pl.when((step >= 1) & (step <= chunks))
+        def _():
             pass_to_core(step - 1)
-        if step == 2:
-            for d in range(1, buckets):
-                landed(src_have.at[(me - d + buckets) % buckets], sr_sem.at[d])
-                landed(count_have.at[(me - d + buckets) % buckets], nr_sem.at[d])
-        if step >= 2:
+
+        @pl.when(step == 2)
+        def _():
+            landed(src_have.at[pl.ds(0, buckets - 1)], sr_sem.at[0])
+            landed(count_have.at[pl.ds(0, buckets - 1)], nr_sem.at[0])
+
+        @pl.when(step >= 2)
+        def _():
             add_scores(step - 2)
+
+        return 0
+
+    lax.fori_loop(0, chunks + 2, one_step, 0)
 
     bwd_have[col] = jnp.zeros(bwd_have.shape[1:], f32)
 
@@ -318,27 +331,27 @@
 
     def bwd_copy(d):
         return remote(
-            bwd_have.at[col], bwd_have.at[col], bs_sem.at[d], br_sem.at[d],
+            bwd_have.at[col], bwd_have.at[col], bs_sem.at[0], br_sem.at[0],
             (me, (col + d) % columns),
         )
 
     def fore_copy(d):
         return remote(
-            fore_have.at[col], fore_have.at[col], fs_sem.at[d], fr_sem.at[d],
+            fore_have.at[col], fore_have.at[col], fs_sem.at[0], fr_sem.at[0],
             (me, (col + d) % columns),
         )
 
     def part_copy(h, d):
         b = (me + d) % buckets
         return remote(
-            part_send.at[h, b], part_have.at[h, me], ps_sem.at[h, d], pr_sem.at[h, d], (b, col)
+            part_send.at[h, b], part_have.at[h, me], ps_sem.at[0], pr_sem.at[0], (b, col)
         )
 
     def partner(d):
         b = (me + d) % buckets
         at = block_of(b)
         scale = safe_ratio(1.0, fwd_total[at, :])
-        for h in range(chunks):
+        def one_piece(h, _):
             acc = jnp.zeros((cap, piece), f32)
             for cu in range(2 * units):
                 acc = acc + jnp.dot(
@@ -352,19 +365,19 @@
             else:
                 part_send[h, b] = done
                 part_copy(h, d).start()
+            return 0
+
+        lax.fori_loop(0, chunks, one_piece, 0)
 
     weigh((me + 1) % buckets)
     partner(1)
-    for d in range(2, buckets + 1):
-        weigh((me + d) % buckets)
+    lax.fori_loop(2, buckets + 1, lambda d, _: (weigh((me + d) % buckets), 0)[1], 0)
     for d in range(1, columns):
         bwd_copy(d).start()
     for d in range(2, buckets):
         partner(d)
-    partner(0)
-
-    for d in range(1, columns):
-        landed(bwd_have.at[(col - d + columns) % columns], br_sem.at[d])
+
+    landed(bwd_have.at[pl.ds(0, columns - 1)], br_sem.at[0])
     bwd_all = bwd_have[0]
     for c in range(1, columns):
         bwd_all = bwd_all + bwd_have[c]
@@ -396,14 +409,14 @@
 
     def smar_copy(d):
         b = (me + d) % buckets
-        return remote(smar_send.at[b], smar_have.at[me], ms_sem.at[d], mr_sem.at[d], (b, col))
+        return remote(smar_send.at[b], smar_have.at[me], ms_sem.at[0], mr_sem.at[0], (b, col))
 
     for d in range(1, buckets):
         smar_copy(d).start()
     smar_have[me] = smar_send[me]
 
-    for d in range(1, columns):
-        landed(fore_have.at[(col - d + columns) % columns], fr_sem.at[d])
+    partner(0)
+    landed(fore_have.at[pl.ds(0, columns - 1)], fr_sem.at[0])
     fore_all = fore_have[0]
     for c in range(1, columns):
         fore_all = fore_all + fore_have[c]
@@ -417,45 +430,39 @@
     def tmar_copy(d):
         b = (me + d) % buckets
         return remote(
-            tmar_send.at[mine, b], tmar_have.at[me], ts_sem.at[d], tr_sem.at[d], (b, col)
+            tmar_send.at[mine, b], tmar_have.at[me], ts_sem.at[0], tr_sem.at[0], (b, col)
         )
 
     for d in range(1, buckets):
         tmar_copy(d).start()
     tmar_have[me] = tmar_send[mine, me]
 
-    for d in range(1, buckets):
-        b = (me - d + buckets) % buckets
-        for h in range(chunks):
-            landed(part_have.at[h, b], pr_sem.at[h, d])
-        landed(smar_have.at[b], mr_sem.at[d])
-        landed(tmar_have.at[b], tr_sem.at[d])
-
-    for d in range(1, line):
-        slot_copy(d).wait_send()
-    for h in range(chunks):
-        for block in range(line):
-            @pl.when((block <= z) & (z + 1 < line))
-            def _():
-                up_copy(block, h).wait_send()
-
-            @pl.when((block >= z) & (z > 0))
-            def _():
-                down_copy(block, h).wait_send()
-        for u in range(units):
-            core_copy(h, u).wait_send()
-        for d in range(1, buckets):
-            part_copy(h, d).wait_send()
-            for u in range(units):
-                x_copy(h, u, d).wait_send()
-    for d in range(1, buckets):
-        src_copy(d).wait_send()
-        count_copy(d).wait_send()
-        smar_copy(d).wait_send()
-        tmar_copy(d).wait_send()
-    for d in range(1, columns):
-        bwd_copy(d).wait_send()
-        fore_copy(d).wait_send()
+    others = pl.ds(0, buckets - 1)
+    landed(part_have.at[:, others], pr_sem.at[0])
+    landed(smar_have.at[others], mr_sem.at[0])
+    landed(tmar_have.at[others], tr_sem.at[0])
+
+    def left(ref, sem):
+        remote(ref, ref, sem, sem, (me, other)).wait_send()
+
+    left(slots.at[pl.ds(0, line - 1)], slot_ssem.at[0])
+    for block in range(line):
+        @pl.when((block <= z) & (z + 1 < line))
+        def _():
+            left(raw.at[block], up_sem.at[block])
+
+        @pl.when((block >= z) & (z > 0))
+        def _():
+            left(raw.at[block], down_sem.at[block])
+    left(src_send.at[others], ss_sem.at[0])
+    left(count_send.at[others], ns_sem.at[0])
+    left(packed.at[:, :, others], xs_sem.at[0])
+    left(every.at[:, core], cs_sem.at[0])
+    left(bwd_have.at[pl.ds(0, columns - 1)], bs_sem.at[0])
+    left(fore_have.at[pl.ds(0, columns - 1)], fs_sem.at[0])
+    left(part_send.at[:, others], ps_sem.at[0])
+    left(smar_send.at[others], ms_sem.at[0])
+    left(tmar_have.at[others], ts_sem.at[0])
 
 
 def on_device(source, source_label, target, target_label):
@@ -490,29 +497,29 @@
         vmem((chunks, buckets, cap, piece), bf16),
         vmem((buckets, 8, 128), f32),
         vmem((2 * units, buckets, 8, 128), f32),
-        dma((line, chunks)),
-        dma((line, chunks)),
-        dma((line, chunks)),
         dma((line,)),
         dma((line,)),
-        dma((chunks, units, buckets)),
-        dma((chunks, units, buckets)),
+        dma((line, chunks)),
+        dma((1,)),
+        dma((1,)),
+        dma((1,)),
         dma((chunks, units)),
+        dma((1,)),
         dma((chunks, units)),
-        dma((buckets,)),
-        dma((buckets,)),
-        dma((buckets,)),
-        dma((buckets,)),
-        dma((columns,)),
-        dma((columns,)),
-        dma((columns,)),
-        dma((columns,)),
-        dma((chunks, buckets)),
-        dma((chunks, buckets)),
-        dma((buckets,)),
-        dma((buckets,)),
-        dma((buckets,)),
-        dma((buckets,)),
+        dma((1,)),
+        dma((1,)),
+        dma((1,)),
+        dma((1,)),
+        dma((1,)),
+        dma((1,)),
+        dma((1,)),
+        dma((1,)),
+        dma((1,)),
+        dma((1,)),
+        dma((1,)),
+        dma((1,)),
+        dma((1,)),
+        dma((1,)),
     ]
     src_row = source_label.reshape(1, rows)
     tgt_row = target_label.reshape(1, rows)

time: 77.6 us -> 76.9 us (level)
  no operation moved by 1% of the time
where the time goes in v6:
time: 76.9 us; the launch traced here: 76.7 us
  Pallas kernels  76.1 us (99%)
    pallas_call x1, Pallas kernels, on_device(): pl.pallas_call(functools.partial(kernel, buckets, columns, cap), out_shap...  73.2 us
    pallas_call x1, Pallas kernels, on_device(): pl.pallas_call(functools.partial(unpack_kernel, buckets, columns, cap), o...  2.94 us

profile of v6, /device:TPU:0, one launch (start us, length us, event | category | flops | bytes accessed | tf_op | source)
XLA Modules:
  0.0 76.7 jit_solution(3336984986349840004)
XLA Ops:
  0.6 73.2 %bitext.1 = (bf16[4,4,128,256]{3,2,1,0:T(8,128)(2,1)}, f32[4,8,128]{2,1,0:T(8,128)}, f32[4,8,128]{2,1,0:T(8,128)}) custom-call(bf16[256,1024]{1,0:T(8,128)(2,1)} %src_ref.1, bf16[256,1024]{1,0:T(8,128)(2,1)} %tgt_ref.1, s32[1,256]{1,0:T(1,128)} %bitcast.4, s32[1,256]{1,0:T(1,128)} %bitcast.6), custom_call_target="tpu_custom_call" | custom-call | tf_op jit(solution)/shard_map/bitext/pallas_call | solution.py:527
  73.8 2.9 %unpack.1 = (f32[256,1024]{1,0:T(8,128)}, f32[1,256]{1,0:T(1,128)}, f32[1,256]{1,0:T(1,128)}) custom-call(s32[1,256]{1,0:T(1,128)} %bitcast.5, s32[1,256]{1,0:T(1,128)} %bitcast.7, bf16[4,4,128,256]{3,2,1,0:T(8,128)(2,1)} %get-tuple-element.9.part_have, f32[4,8,128]{2,1,0:T(8,128)} %get-tuple-element.10.smar_have, f32[4,8,128]{2,1,0:T(8,128)} %get-tuple-element.11.tmar_have), custom_call_target="tpu_custom_call" | custom-call | tf_op jit(solution)/shard_map/unpack/pallas_call | solution.py:542

commit v7 on v6

--- a/solution.py
+++ b/solution.py
@@ -57,10 +57,9 @@
     tgt_slot = target_slot(tgt_row[...], cap, front)
     slot_col = to_column(src_slot).astype(jnp.int32)
     unpick = (iota((rows, slot_total), 1) == slot_col).astype(bf16)
-    for h in range(chunks):
-        out_ref[:, h * piece:(h + 1) * piece] = jnp.dot(
-            unpick, part_have[h].reshape(slot_total, piece), preferred_element_type=f32
-        )
+    out_ref[...] = jnp.dot(
+        unpick, part_have[0].reshape(slot_total, piece), preferred_element_type=f32
+    )
 
     def spread(have, slot):
         total = jnp.zeros((8, rows), f32)
@@ -72,8 +71,10 @@
             )
         return total[0:1]
 
-    src_out[...] = spread(smar_have, src_slot)
-    tgt_out[...] = spread(tmar_have, tgt_slot)
+    @pl.when(pl.program_id(0) == 0)
+    def _():
+        src_out[...] = spread(smar_have, src_slot)
+        tgt_out[...] = spread(tmar_have, tgt_slot)
 
 
 def kernel(
@@ -347,35 +348,36 @@
             part_send.at[h, b], part_have.at[h, me], ps_sem.at[0], pr_sem.at[0], (b, col)
         )
 
-    def partner(d):
-        b = (me + d) % buckets
-        at = block_of(b)
-        scale = safe_ratio(1.0, fwd_total[at, :])
+    def partner(places):
+        ats = [block_of((me + d) % buckets) for d in places]
+        scale = safe_ratio(1.0, jnp.concatenate([fwd_total[at, :] for at in ats], axis=0))
+
         def one_piece(h, _):
-            acc = jnp.zeros((cap, piece), f32)
+            acc = jnp.zeros((len(places) * cap, piece), f32)
             for cu in range(2 * units):
                 acc = acc + jnp.dot(
-                    weights[cu, at, :],
+                    jnp.concatenate([weights[cu, at, :] for at in ats], axis=0),
                     every[h, cu // units, cu % units].reshape(slot_total, piece),
                     preferred_element_type=f32,
                 )
             done = (acc * scale).astype(bf16)
-            if d == 0:
-                part_have[h, me] = done
-            else:
-                part_send[h, b] = done
-                part_copy(h, d).start()
+            for t, d in enumerate(places):
+                block = done[t * cap:(t + 1) * cap]
+                if d == buckets:
+                    part_have[h, me] = block
+                else:
+                    part_send[h, (me + d) % buckets] = block
+                    part_copy(h, d).start()
             return 0
 
         lax.fori_loop(0, chunks, one_piece, 0)
 
     weigh((me + 1) % buckets)
-    partner(1)
+    partner([1])
     lax.fori_loop(2, buckets + 1, lambda d, _: (weigh((me + d) % buckets), 0)[1], 0)
     for d in range(1, columns):
         bwd_copy(d).start()
-    for d in range(2, buckets):
-        partner(d)
+    partner(list(range(2, buckets + 1)))
 
     landed(bwd_have.at[pl.ds(0, columns - 1)], br_sem.at[0])
     bwd_all = bwd_have[0]
@@ -415,7 +417,6 @@
         smar_copy(d).start()
     smar_have[me] = smar_send[me]
 
-    partner(0)
     landed(fore_have.at[pl.ds(0, columns - 1)], fr_sem.at[0])
     fore_all = fore_have[0]
     for c in range(1, columns):
@@ -546,8 +547,19 @@
             jax.ShapeDtypeStruct((1, rows), f32),
             jax.ShapeDtypeStruct((1, rows), f32),
         ),
-        in_specs=[whole] * 5,
-        out_specs=(whole,) * 3,
+        grid=(chunks,),
+        in_specs=[
+            pl.BlockSpec((1, rows), lambda h: (0, 0)),
+            pl.BlockSpec((1, rows), lambda h: (0, 0)),
+            pl.BlockSpec((1, buckets, cap, piece), lambda h: (h, 0, 0, 0)),
+            pl.BlockSpec((buckets, 8, 128), lambda h: (0, 0, 0)),
+            pl.BlockSpec((buckets, 8, 128), lambda h: (0, 0, 0)),
+        ],
+        out_specs=(
+            pl.BlockSpec((rows, piece), lambda h: (0, h)),
+            pl.BlockSpec((1, rows), lambda h: (0, 0)),
+            pl.BlockSpec((1, rows), lambda h: (0, 0)),
+        ),
         name="unpack",
     )(src_row, tgt_row, part_have, smar_have, tmar_have)
     return (partner, src_out.reshape(rows), tgt_out.reshape(rows))

time: 76.9 us -> 78.8 us (1.025)
  Pallas kernels: 76.1 us -> 78 us
    pallas_call x1, Pallas kernels: 2.94 us -> 4.83 us  [on_device(): pl.pallas_call(functools.partial(unpack_kernel, buckets, columns, cap), o...]
where the time goes in v7:
time: 78.8 us; the launch traced here: 78.6 us
  Pallas kernels  78 us (99%)
    pallas_call x1, Pallas kernels, on_device(): pl.pallas_call(functools.partial(kernel, buckets, columns, cap), out_shap...  73.2 us
    pallas_call x1, Pallas kernels, on_device(): pl.pallas_call(functools.partial(unpack_kernel, buckets, columns, cap), o...  4.83 us

profile of v7, /device:TPU:0, one launch (start us, length us, event | category | flops | bytes accessed | tf_op | source)
XLA Modules:
  0.0 78.6 jit_solution(4353661874493875723)
XLA Ops:
  0.6 73.2 %bitext.1 = (bf16[4,4,128,256]{3,2,1,0:T(8,128)(2,1)}, f32[4,8,128]{2,1,0:T(8,128)}, f32[4,8,128]{2,1,0:T(8,128)}) custom-call(bf16[256,1024]{1,0:T(8,128)(2,1)} %src_ref.1, bf16[256,1024]{1,0:T(8,128)(2,1)} %tgt_ref.1, s32[1,256]{1,0:T(1,128)} %bitcast.4, s32[1,256]{1,0:T(1,128)} %bitcast.6), custom_call_target="tpu_custom_call" | custom-call | tf_op jit(solution)/shard_map/bitext/pallas_call | solution.py:528
  73.8 4.8 %unpack.1 = (f32[256,1024]{1,0:T(8,128)}, f32[1,256]{1,0:T(1,128)}, f32[1,256]{1,0:T(1,128)}) custom-call(s32[1,256]{1,0:T(1,128)} %bitcast.5, s32[1,256]{1,0:T(1,128)} %bitcast.7, bf16[4,4,128,256]{3,2,1,0:T(8,128)(2,1)} %get-tuple-element.9.part_have, f32[4,8,128]{2,1,0:T(8,128)} %get-tuple-element.10.smar_have, f32[4,8,128]{2,1,0:T(8,128)} %get-tuple-element.11.tmar_have), custom_call_target="tpu_custom_call" | custom-call | tf_op jit(solution)/shard_map/unpack/pallas_call | solution.py:543

commit v8 on v6

--- a/solution.py
+++ b/solution.py
@@ -135,24 +135,19 @@
 
     def up_copy(block, h):
         return remote(
-            raw.at[block, h], raw.at[block, h], up_sem.at[block],
-            block_sem.at[block, h], (me, jnp.minimum(z + 1, line - 1) * 2 + core),
+            raw.at[block, h], raw.at[block, h], up_sem.at[0],
+            block_sem.at[block, h], (me, ((z + 1) % line) * 2 + core),
         )
 
     def down_copy(block, h):
         return remote(
-            raw.at[block, h], raw.at[block, h], down_sem.at[block],
-            block_sem.at[block, h], (me, jnp.maximum(z - 1, 0) * 2 + core),
+            raw.at[block, h], raw.at[block, h], down_sem.at[0],
+            block_sem.at[block, h], (me, ((z - 1 + line) % line) * 2 + core),
         )
 
     def send_own(h):
-        @pl.when(z + 1 < line)
-        def _():
-            up_copy(z, h).start()
-
-        @pl.when(z > 0)
-        def _():
-            down_copy(z, h).start()
+        up_copy(z, h).start()
+        down_copy(z, h).start()
 
     send_own(0)
     send_own(1)
@@ -202,7 +197,7 @@
         )
 
     def unit_at(t):
-        return jnp.where(z < units, t, units - 1 - t)
+        return (z + units - 1 - t) % units
 
     def pack_unit(h, u):
         block = jnp.dot(picks[u], raw[u, h], preferred_element_type=f32) + jnp.dot(
@@ -213,40 +208,32 @@
             x_copy(h, u, d).start()
         every[h, core, u, me] = packed[h, u, me]
 
-    def pack_ready(h, s):
-        lower = z < units
-        if s < line - 1 and s >= units:
-            u = jnp.where(lower, s - units, line - 1 - s)
-            pack_unit(h, u)
-        if s == line - 1:
-            for t in range(units - 1, units):
-                pack_unit(h, jnp.where(lower, t, units - 1 - t))
-
     def gather_blocks(h):
         @pl.when(h + 2 < chunks)
         def _():
             send_own(h + 2)
 
-        for s in range(1, line):
-            @pl.when(z - s >= 0)
+        for s in range(1, units):
+            below = (z - s + line) % line
+            landed(raw.at[below, h], block_sem.at[below, h])
+
+            @pl.when((s + 1 < units) | (h % 2 == 0))
             def _():
-                block = jnp.maximum(z - s, 0)
-                landed(raw.at[block, h], block_sem.at[block, h])
-
-                @pl.when(z + 1 < line)
-                def _():
-                    up_copy(block, h).start()
-
-            @pl.when(z + s < line)
+                up_copy(below, h).start()
+
+            above = (z + s) % line
+            landed(raw.at[above, h], block_sem.at[above, h])
+
+            @pl.when((s + 1 < units) | (h % 2 == 1))
             def _():
-                block = jnp.minimum(z + s, line - 1)
-                landed(raw.at[block, h], block_sem.at[block, h])
-
-                @pl.when(z > 0)
-                def _():
-                    down_copy(block, h).start()
-
-            pack_ready(h, s)
+                down_copy(above, h).start()
+
+            for j in range(units):
+                if max(j, units - j) == s:
+                    pack_unit(h, (z + j) % units)
+        far = (z + units) % line
+        landed(raw.at[far, h], block_sem.at[far, h])
+        pack_unit(h, z % units)
 
     def pass_to_core(h):
         for t in range(units):
@@ -446,14 +433,9 @@
         remote(ref, ref, sem, sem, (me, other)).wait_send()
 
     left(slots.at[pl.ds(0, line - 1)], slot_ssem.at[0])
-    for block in range(line):
-        @pl.when((block <= z) & (z + 1 < line))
-        def _():
-            left(raw.at[block], up_sem.at[block])
-
-        @pl.when((block >= z) & (z > 0))
-        def _():
-            left(raw.at[block], down_sem.at[block])
+    for sem in (up_sem, down_sem):
+        left(raw.at[pl.ds(0, units - 1)], sem.at[0])
+        left(raw.at[0, pl.ds(0, chunks // 2)], sem.at[0])
     left(src_send.at[others], ss_sem.at[0])
     left(count_send.at[others], ns_sem.at[0])
     left(packed.at[:, :, others], xs_sem.at[0])

time: 76.9 us -> 82.4 us (1.072)
  Pallas kernels: 76.1 us -> 81.6 us
    pallas_call x1, Pallas kernels: 73.2 us -> 78.7 us  [on_device(): pl.pallas_call(functools.partial(kernel, buckets, columns, cap), out_shap...]
where the time goes in v8:
time: 82.4 us; the launch traced here: 82.3 us
  Pallas kernels  81.6 us (99%)
    pallas_call x1, Pallas kernels, on_device(): pl.pallas_call(functools.partial(kernel, buckets, columns, cap), out_shap...  78.7 us
    pallas_call x1, Pallas kernels, on_device(): pl.pallas_call(functools.partial(unpack_kernel, buckets, columns, cap), o...  2.94 us

profile of v8, /device:TPU:0, one launch (start us, length us, event | category | flops | bytes accessed | tf_op | source)
XLA Modules:
  0.0 82.3 jit_solution(1390392860313241587)
XLA Ops:
  0.6 78.7 %bitext.1 = (bf16[4,4,128,256]{3,2,1,0:T(8,128)(2,1)}, f32[4,8,128]{2,1,0:T(8,128)}, f32[4,8,128]{2,1,0:T(8,128)}) custom-call(bf16[256,1024]{1,0:T(8,128)(2,1)} %src_ref.1, bf16[256,1024]{1,0:T(8,128)(2,1)} %tgt_ref.1, s32[1,256]{1,0:T(1,128)} %bitcast.4, s32[1,256]{1,0:T(1,128)} %bitcast.6), custom_call_target="tpu_custom_call" | custom-call | tf_op jit(solution)/shard_map/bitext/pallas_call | solution.py:509
  79.3 2.9 %unpack.1 = (f32[256,1024]{1,0:T(8,128)}, f32[1,256]{1,0:T(1,128)}, f32[1,256]{1,0:T(1,128)}) custom-call(s32[1,256]{1,0:T(1,128)} %bitcast.5, s32[1,256]{1,0:T(1,128)} %bitcast.7, bf16[4,4,128,256]{3,2,1,0:T(8,128)(2,1)} %get-tuple-element.9.part_have, f32[4,8,128]{2,1,0:T(8,128)} %get-tuple-element.10.smar_have, f32[4,8,128]{2,1,0:T(8,128)} %get-tuple-element.11.tmar_have), custom_call_target="tpu_custom_call" | custom-call | tf_op jit(solution)/shard_map/unpack/pallas_call | solution.py:524
